TPU v7x, 128 devices: a whole 4x4x4 slice. The times are simulated.
128 devices in a mesh: rows: 128 (over x, y, z, core).
Axes of the slice: x: 4, y: 4, z: 4, core: 2. Of those that a mesh axis runs over, the one named last changes fastest.
Arguments:
- tokens: float32 [128, 1024, 256], P('rows'), may hold values from -6 to 6
- stored: float32 [128, 1024, 256], P('rows'), may hold values from -6 to 6
- upstream: float32 [128, 1024, 256], P('rows'), may hold values from -6 to 6
- drop_attn: int32 [128, 14, 1024], P('rows'), may hold values from 0 to 524287
- drop_ffn: int32 [128, 14, 1024], P('rows'), may hold values from 0 to 524287
- depth_keep: int32 [2, 16, 128], replicated, may hold values 0 or 1
- gain_one: float32 [256], replicated, may hold values from 0.1 to 1.9
- shift_one: float32 [256], replicated, may hold values from -3 to 3
- w_qkv: float32 [256, 768], replicated, as said below
- w_out: float32 [256, 256], replicated, may hold values from -0.375 to 0.375
- gain_two: float32 [256], replicated, may hold values from 0.1 to 1.9
- shift_two: float32 [256], replicated, may hold values from -3 to 3
- w_up: float32 [256, 1024], replicated, may hold values from -0.375 to 0.375
- up_bias: float32 [1024], replicated, may hold values from -3 to 3
- w_down: float32 [1024, 256], replicated, may hold values from -0.1875 to 0.1875
Outputs:
- result: float32 [128, 1024, 256], P('rows')
- grad_gain_one: float32 [256], replicated
- grad_shift_one: float32 [256], replicated
- grad_w_qkv: float32 [256, 768], replicated
- grad_w_out: float32 [256, 256], replicated
- grad_gain_two: float32 [256], replicated
- grad_shift_two: float32 [256], replicated
- grad_w_up: float32 [256, 1024], replicated
- grad_up_bias: float32 [1024], replicated
- grad_w_down: float32 [1024, 256], replicated
Inputs may be any that keep to these rules, and one draw needn't show every extreme that they name: `w_qkv`: columns are the queries, then the keys, then the values, each head's 32 columns together.
All inputs are finite; a program needn't handle non-finite values.
Results may differ from a plain program's by a relative error of at most 0.0003.
Values sent between devices are 32-bit elements; how exact they have to be, the bound alone decides.
A program may use at most 384 MiB of HBM per device.

v0:
```python
from functools import partial

import jax
import jax.numpy as jnp
from jax import lax
from jax.sharding import PartitionSpec as P

NH = 8


PRECISE = lax.Precision.HIGHEST
EPSILON = 1e-05
KEEP_SCALE = 8.0 / 3.0


def layer_norm(inputs, scales, offsets):
    average = jnp.mean(inputs, -1, keepdims=True)
    centred = inputs - average
    spread = jnp.mean(centred * centred, -1, keepdims=True)
    return centred * lax.rsqrt(spread + EPSILON) * scales + offsets


def attend(queries, keys_in, values_in, layout):
    key_layout = layout.replace("i", "k").replace("j", "l")
    scores = jnp.einsum(
        layout + "," + key_layout + "->abnijkl", queries, keys_in, precision=PRECISE
    )
    scores = scores * queries.shape[-1] ** (-0.5)
    score_shape = scores.shape
    weights = jax.nn.softmax(scores.reshape(score_shape[:5] + (-1,)), axis=-1).reshape(score_shape)
    return jnp.einsum(
        "abnijkl," + key_layout + "->" + layout, weights, values_in, precision=PRECISE
    )


def attention_branch(layout, grid_tokens, gain_one, shift_one, w_qkv, w_out):
    normed = layer_norm(grid_tokens, gain_one, shift_one)
    projected = jnp.einsum("...c,ce->...e", normed, w_qkv, precision=PRECISE)
    parts = projected.reshape(projected.shape[:-1] + (3, NH, w_qkv.shape[0] // NH))
    mixed = attend(parts[..., 0, :, :], parts[..., 1, :, :], parts[..., 2, :, :], layout)
    merged = mixed.reshape(mixed.shape[:-2] + (w_out.shape[0],))
    return jnp.einsum("...c,ce->...e", merged, w_out, precision=PRECISE)


def ffn_branch(stored, gain_two, shift_two, w_up, up_bias, w_down):
    normed = layer_norm(stored, gain_two, shift_two)
    hidden = jax.nn.gelu(
        jnp.einsum("...c,cf->...f", normed, w_up, precision=PRECISE) + up_bias, approximate=False
    )
    return jnp.einsum("...f,fc->...c", hidden, w_down, precision=PRECISE)


def unpack(packed, channels):
    channel_ids = jnp.arange(channels, dtype=jnp.int32)
    picked = jnp.take(packed, channel_ids // 19, axis=1)
    bit_values = jnp.right_shift(picked, (channel_ids % 19)[None, :, None]) & 1
    return jnp.transpose(bit_values, (0, 2, 1)).astype(jnp.float32)


def direct_out(band_tokens, devices):
    band_rows, columns, channels = band_tokens.shape
    shaped = band_tokens.reshape(band_rows, 8, devices, columns // (8 * devices), channels)
    moved = lax.all_to_all(shaped, "rows", split_axis=2, concat_axis=0, tiled=True)
    return moved.reshape(8, devices * band_rows // 8, 8, columns // (8 * devices), channels)


def direct_back(grid_tokens, band_rows):
    group_cols = grid_tokens.shape[3]
    channels = grid_tokens.shape[4]
    shaped = grid_tokens.reshape(-1, 8, 1, group_cols, channels)
    moved = lax.all_to_all(shaped, "rows", split_axis=0, concat_axis=2, tiled=True)
    return moved.reshape(band_rows, -1, channels)


def local(
    tokens,
    stored,
    upstream,
    drop_attn,
    drop_ffn,
    depth_keep,
    gain_one,
    shift_one,
    w_qkv,
    w_out,
    gain_two,
    shift_two,
    w_up,
    up_bias,
    w_down,
):
    band_rows, columns, channels = tokens.shape
    devices = lax.axis_size("rows")
    position = lax.axis_index("rows")
    grad_scale = float(band_rows * columns * devices) ** (-0.5)
    flag_row = lax.dynamic_index_in_dim(depth_keep, position * band_rows // 8, 1, keepdims=False)
    flag_cols = jnp.repeat(flag_row, 8, axis=1).astype(jnp.float32)
    factor_attn = unpack(drop_attn, channels) * flag_cols[0][None, :, None] * KEEP_SCALE
    factor_ffn = unpack(drop_ffn, channels) * flag_cols[1][None, :, None] * KEEP_SCALE
    grid_in = direct_out(tokens, devices)
    layout = "iajbnd"
    ffn_value, ffn_back = jax.vjp(ffn_branch, stored, gain_two, shift_two, w_up, up_bias, w_down)
    ffn_grads = ffn_back(upstream * factor_ffn)
    through = upstream + ffn_grads[0]
    branch_grad = through * factor_attn
    grid_grad = direct_out(branch_grad, devices)
    attn_value, attn_back = jax.vjp(
        partial(attention_branch, layout), grid_in, gain_one, shift_one, w_qkv, w_out
    )
    attn_grads = attn_back(grid_grad)
    back_band = direct_back(attn_grads[0], band_rows)
    result = through + back_band
    totals = lax.psum(
        (
            attn_grads[1] * grad_scale,
            attn_grads[2] * grad_scale,
            attn_grads[3] * grad_scale,
            attn_grads[4] * grad_scale,
            ffn_grads[1] * grad_scale,
            ffn_grads[2] * grad_scale,
            ffn_grads[3] * grad_scale,
            ffn_grads[4] * grad_scale,
            ffn_grads[5] * grad_scale,
        ),
        "rows",
    )
    return (
        result,
        totals[0],
        totals[1],
        totals[2],
        totals[3],
        totals[4],
        totals[5],
        totals[6],
        totals[7],
        totals[8],
    )


def solution(mesh):
    placed = (
        P("rows", None, None),
        P("rows", None, None),
        P("rows", None, None),
        P("rows", None, None),
        P("rows", None, None),
        P(),
        P(),
        P(),
        P(),
        P(),
        P(),
        P(),
        P(),
        P(),
        P(),
    )
    return jax.shard_map(
        local,
        mesh=mesh,
        in_specs=placed,
        out_specs=(P("rows", None, None), P(), P(), P(), P(), P(), P(), P(), P(), P()),
        check_vma=False,
    )
```

profile of v0, /device:TPU:1, one launch (start us, length us, event | category | flops | bytes accessed | tf_op | source)
XLA Modules:
  0.0 785.7 jit_solution(1096289215075389679)
XLA Ops:
  7.2 2.9 copy.95
  10.2 11.5 %all-to-all-start.1 = ((f32[1,8,128,1,256]{4,1,3,0,2:T(8,128)}), f32[1,8,128,1,256]{4,1,3,0,2:T(8,128)S(1)}, u32[]{:S(2)}, u32[]{:S(2)}) async-start(f32[1,8,128,1,256]{4,1,3,0,2:T(8,128)} %copy.95), calls=%async_computation.1 | async-start | bytes 2097152 | tf_op jit(solution)/shard_map/all_to_all | solution.py:63
  21.8 0.7 dynamic-slice_convert_fusion
  22.5 0.2 reduce_sum.132
  22.7 0.4 multiply_reduce_fusion.5
  23.1 0.1 broadcast_in_dim.31
  23.2 0.1 mul.318
  23.3 0.1 broadcast_in_dim.62
  23.3 0.1 mul.343
  23.5 2.0 gather_fusion
  25.5 2.6 copy.92
  28.1 2.0 gather_fusion.1
  30.1 2.5 copy.93
  32.7 12.4 %fusion.3 = (f32[1024,1024]{1,0:T(8,128)S(1)}, f32[1024,1024]{1,0:T(8,128)S(1)}) fusion(f32[1024]{0:T(1024)S(1)} %copy-done.40, f32[256,1024]{1,0:T(8,128)S(1)} %copy-done, f32[1,1024,256]{2,1,0:T(8,128)S(1)} %copy-done.7, f32[256]{0:T(256)S(1)} %copy-done.44, f32[256]{0:T(256)S(1)} %copy-done.39, f32[1024]{0:T(1024)S(1)} %fusion.78, ...), kind=kOutput, calls=%fused_computation.13 | convolution fusion | flops 3288334336 | bytes 10500096 | tf_op jit(solution)/shard_map/jvp(...c,cf->...f)/dot_general | solution.py:48
  45.2 6.0 fusion.85
  51.2 4.3 fusion.48
  55.6 0.6 fusion.84
  56.2 0.3 copy-done.15
  56.6 0.7 copy-done.35
  57.2 1.3 bitcast_multiply_fusion.1
  58.6 2.3 copy.96
  60.9 3.0 copy.94
  63.8 7.1 convolution_multiply_fusion
  70.9 10.4 %fusion.43 = f32[1024,256]{1,0:T(8,128)} fusion(f32[1024,1024]{1,0:T(8,128)S(1)} %copy-done.21, f32[1024,1024]{1,0:T(8,128)} %copy-done.22, f32[1024]{0:T(1024)S(1)} %copy-done.40, f32[1,1024,256]{2,1,0:T(8,128)S(1)} %copy-done.13, s32[256,1024]{0,1:T(8,128)S(1)} %copy-done.26, f32[1024]{0:T(1024)S(1)} %mul.318, s32[256]{0:T(256)S(1)} %and_select_fusion, ...), kind=kOutput, calls=%fused_computation.59 | convolution fusion | flops 3226468352 | bytes 11543808 | tf_op jit(solution)/shard_map/transpose(jvp(...f,fc->...c))/dot_general | solution.py:50
  81.3 9.8 %all-to-all-start = ((f32[1,8,128,1,256]{4,1,3,0,2:T(8,128)}), f32[1,8,128,1,256]{4,1,3,0,2:T(8,128)S(1)}, u32[]{:S(2)}, u32[]{:S(2)}) async-start(f32[1,8,128,1,256]{4,1,3,0,2:T(8,128)} %copy.94), calls=%async_computation | async-start | bytes 2097152 | tf_op jit(solution)/shard_map/all_to_all | solution.py:63
  91.1 0.0 all-reduce.7.cloned.1.call-start
  91.1 0.2 bitcast_reduce_fusion
  91.4 0.4 multiply_reduce_fusion.4
  91.8 0.6 multiply_add_fusion.5
  92.4 0.3 multiply_add_fusion.1
  92.8 13.6 %convolution_bitcast_fusion = f32[8,16,8,1,3,8,32]{6,2,5,4,1,0,3:T(8,128)} fusion(f32[8,16,8,256,1,1]{3,2,5,4,1,0:T(8,128)S(1)} %bitcast.245, f32[3,8,32,256,1,1]{3,2,1,0,5,4:T(8,128)} %bitcast.252), kind=kOutput, calls=%fused_computation.12 | convolution fusion | flops 2415919104 | bytes 4980736 | tf_op jit(solution)/shard_map/jvp(...c,ce->...e)/dot_general | solution.py:38
  106.4 10.1 %slice_bitcast_fusion.1 = (f32[8,16,8,8,32,1]{4,2,3,1,0,5:T(8,128)}, f32[8,16,8,8,32,1]{4,2,3,1,0,5:T(8,128)}, f32[8,16,8,8,32,1]{4,2,3,1,0,5:T(8,128)}) fusion(f32[8,16,8,1,3,8,32]{6,2,5,4,1,0,3:T(8,128)} %convolution_bitcast_fusion), kind=kLoop, calls=%fused_computation.15 | loop fusion | bytes 6291456 | tf_op jit(solution)/shard_map/reshape.70
  116.5 78.8 %multiply_reduce_fusion.1 = (f32[16,8,8,8]{3,2,1,0:T(8,128)S(1)}, f32[16,8,8,8,8,8]{3,5,4,2,1,0:T(8,128)}) fusion(f32[8,16,8,8,32,1]{4,2,3,1,0,5:T(8,128)} %get-tuple-element.30, f32[8,16,8,8,32,1]{4,2,3,1,0,5:T(8,128)} %get-tuple-element.32), kind=kOutput, calls=%fused_computation.7 | convolution fusion | flops 202366976 | bytes 4227072 | tf_op jit(solution)/shard_map/jvp(iajbnd,kalbnd->abnijkl)/dot_general | solution.py:25
  195.3 15.0 %fusion.2 = f32[16,8,8,8]{3,2,1,0:T(8,128)S(1)} fusion(f32[16,8,8,8]{3,2,1,0:T(8,128)S(1)} %get-tuple-element.39, f32[16,8,8,8,8,8]{3,5,4,2,1,0:T(8,128)} %get-tuple-element.40), kind=kLoop, calls=%fused_computation.9 | loop fusion | flops 1564672 | bytes 2162688 | tf_op jit(solution)/shard_map/jvp()/reduce_sum | solution.py:30
  210.3 0.1 multiply_divide_fusion
  210.4 4.9 convolution_bitcast_fusion.1
  215.3 83.7 %multiply_reduce_fusion = (f32[16,8,8,8]{3,2,1,0:T(8,128)S(1)}, f32[16,8,8,8,8,8]{3,5,4,2,1,0:T(8,128)}) fusion(f32[16,8,8,8]{3,2,1,0:T(8,128)S(1)} %multiply_divide_fusion, f32[16,8,8,8]{3,2,1,0:T(8,128)S(1)} %get-tuple-element.39, f32[16,8,8,8,8,8]{3,5,4,2,1,0:T(8,128)} %get-tuple-element.40, f32[8,16,8,8,32,1]{4,2,3,1,0,5:T(8,128)} %get-tuple-element.31, ...), kind=kOutput, calls=%fused_computation.5 | convolution fusion | flops 203939840 | bytes 6389760 | tf_op jit(solution)/shard_map/transpose(jvp(abnijkl,kalbnd->iajbnd))/dot_general | solution.py:31
  299.1 45.8 %broadcast_divide_fusion = (f32[16,8,8,8,8,8]{3,5,4,2,1,0:T(8,128)}, f32[16,8,8,8,8,8]{3,5,4,2,1,0:T(8,128)}) fusion(f32[16,8,8,8]{3,2,1,0:T(8,128)S(1)} %fusion.2, f32[16,8,8,8]{3,2,1,0:T(8,128)S(1)} %get-tuple-element.39, f32[16,8,8,8,8,8]{3,5,4,2,1,0:T(8,128)} %get-tuple-element.40, f32[16,8,8,8]{3,2,1,0:T(8,128)S(1)} %neg.29, ...), kind=kLoop, calls=%fused_computation.8 | loop fusion | flops 3670016 | bytes 8486912 | tf_op jit(solution)/shard_map/jvp()/div | solution.py:30
  344.9 57.1 %fusion.38 = f32[8,16,8,1,8,32]{5,2,0,4,1,3:T(8,128)} fusion(f32[16,8,8,8,8,8]{3,5,4,2,1,0:T(8,128)} %get-tuple-element.28, f32[8,16,8,8,32,1]{4,2,3,1,0,5:T(8,128)S(1)} %copy-done.3), kind=kOutput, calls=%fused_computation.53 | convolution fusion | flops 201326592 | bytes 4194304 | tf_op jit(solution)/shard_map/jvp(abnijkl,kalbnd->iajbnd)/dot_general | solution.py:31
  402.0 51.1 %fusion.33 = f32[8,16,8,1,1,8,32]{6,2,0,5,1,4,3:T(8,128)} fusion(f32[16,8,8,8,8,8]{3,5,4,2,1,0:T(8,128)} %get-tuple-element.28, f32[16,8,32,8,8,1]{2,4,1,0,3,5:T(8,128)S(1)} %copy-done.2), kind=kOutput, calls=%fused_computation.51 | convolution fusion | flops 201326592 | bytes 4194304 | tf_op jit(solution)/shard_map/transpose(jvp(abnijkl,kalbnd->iajbnd))/dot_general | solution.py:31
  453.1 57.1 %fusion.27 = f32[8,16,8,1,1,8,32]{6,2,0,5,1,4,3:T(8,128)} fusion(f32[16,8,8,8,8,8]{3,5,4,2,1,0:T(8,128)} %get-tuple-element.29, f32[8,16,8,8,32,1]{4,2,3,1,0,5:T(8,128)S(1)} %copy-done.6), kind=kOutput, calls=%fused_computation.49 | convolution fusion | flops 201326592 | bytes 4194304 | tf_op jit(solution)/shard_map/transpose(jvp(iajbnd,kalbnd->abnijkl))/dot_general | solution.py:25
  510.2 36.0 %fusion.30 = f32[8,16,8,1,1,8,32]{6,2,0,5,1,4,3:T(8,128)} fusion(f32[16,8,8,8,8,8]{3,5,4,2,1,0:T(8,128)} %get-tuple-element.29, f32[8,16,8,8,32,1]{4,2,3,1,0,5:T(8,128)} %get-tuple-element.32), kind=kOutput, calls=%fused_computation.50 | convolution fusion | flops 201326592 | bytes 4194304 | tf_op jit(solution)/shard_map/transpose(jvp(iajbnd,kalbnd->abnijkl))/dot_general | solution.py:25
  546.2 6.6 copy.112
  552.8 3.3 reshape.529
  556.1 12.2 %pad_add_fusion = f32[8,16,8,1,3,8,32]{6,2,0,5,1,4,3:T(8,128)} fusion(f32[8,16,8,1,1,8,32]{6,2,0,5,1,4,3:T(8,128)} %fusion.27, f32[8,16,8,1,1,8,32]{6,2,0,5,1,4,3:T(8,128)} %fusion.30, f32[8,16,8,1,1,8,32]{6,2,0,5,1,4,3:T(8,128)} %fusion.33), kind=kLoop, calls=%fused_computation.10 | loop fusion | flops 1572864 | bytes 6291456 | tf_op jit(solution)/shard_map/transpose(jvp())/add_any | solution.py:40
  568.3 16.3 %copy.107 = f32[8,16,8,1,3,8,32]{6,5,4,2,1,0,3:T(8,128)} copy(f32[8,16,8,1,3,8,32]{6,2,0,5,1,4,3:T(8,128)} %pad_add_fusion) | data formatting | bytes 6291456 | tf_op jit(solution)/shard_map/transpose(jvp())/add_any | solution.py:40
  584.7 9.9 %reshape.525 = f32[8,16,8,768]{3,2,1,0:T(8,128)} reshape(f32[8,16,8,1,3,8,32]{6,5,4,2,1,0,3:T(8,128)} %copy.107) | data formatting | bytes 6291456 | tf_op jit(solution)/shard_map/reshape.93
  594.6 5.7 fusion.46
  600.4 2.8 fusion.83
  603.3 0.9 copy-done.16
  604.2 0.7 multiply_reduce_fusion.2
  604.9 2.6 fusion.47
  607.4 0.0 all-reduce.7.cloned.1.call-update
  607.5 2.7 broadcast_add_fusion
  610.1 9.8 %all-to-all-start.2 = ((f32[128,8,1,1,256]{4,1,3,2,0:T(8,128)}), f32[128,8,1,1,256]{4,1,3,2,0:T(8,128)S(1)}, u32[]{:S(2)}, u32[]{:S(2)}) async-start(f32[128,8,1,1,256]{4,1,3,2,0:T(8,128)} %bitcast.248), calls=%async_computation.2 | async-start | bytes 2097152 | tf_op jit(solution)/shard_map/all_to_all | solution.py:71
  619.9 1.4 reduce_sum.154
  621.3 71.3 %all-reduce.3 = (f32[256]{0:T(256)}, f32[256]{0:T(256)}, f32[256]{0:T(256)}, f32[256]{0:T(256)}, f32[1024]{0:T(1024)}) all-reduce(f32[256]{0:T(256)S(1)} %get-tuple-element.50, f32[256]{0:T(256)S(1)} %broadcast_multiply_fusion.5, f32[256]{0:T(256)S(1)} %get-tuple-element.49, ...), channel_id=1, replica_groups=mesh['rows'=128] {'rows'}, use_global_device_ids=true, to_apply=%region_12.14 | all-reduce | flops 2048 | bytes 16384 | tf_op jit(solution)/shard_map/psum | solution.py:113
  692.6 0.3 copy.109
  693.0 1.2 bitcast_add_fusion
  694.2 77.1 %all-reduce.7.cloned.1.call-done = (f32[256,768]{1,0:T(8,128)}, f32[256,256]{1,0:T(8,128)}, f32[256,1024]{1,0:T(8,128)}, f32[1024,256]{1,0:T(8,128)}) async-done(((f32[256,768]{1,0:T(8,128)}, f32[256,256]{1,0:T(8,128)}, f32[256,1024]{1,0:T(8,128)}, f32[1024,256]{1,0:T(8,128)}), (f32[256,768]{1,0:T(8,128)}, f32[256,256]{1,0:T(8,128)}, f32[256,1024]{1,0:T(8,128)}, ...) | async-done | bytes 3145744 | tf_op jit(solution)/shard_map/psum | solution.py:113
  771.4 2.2 copy.198
  773.5 1.7 copy.199
  775.2 2.3 copy.200
  777.5 1.0 copy.201
  (111 shorter events, 0.4 us)
Async XLA Ops:
  7.2 25.5 %copy-start = (f32[256,1024]{1,0:T(8,128)S(1)}, f32[256,1024]{1,0:T(8,128)}, u32[]{:S(2)}) copy-start(f32[256,1024]{1,0:T(8,128)} %param.29) | copy-start | bytes 3145732
  7.2 15.3 %copy-start.7 = (f32[1,1024,256]{2,1,0:T(8,128)S(1)}, f32[1,1024,256]{2,1,0:T(8,128)}, u32[]{:S(2)}) copy-start(f32[1,1024,256]{2,1,0:T(8,128)} %param.18) | copy-start | bytes 3145732
  7.2 16.2 %copy-start.33 = (s32[1,14,1024]{2,0,1:T(1,128)S(1)}, s32[1,14,1024]{2,0,1:T(1,128)}, u32[]{:S(2)}) copy-start(s32[1,14,1024]{2,0,1:T(1,128)} %param.20) | copy-start | bytes 172036
  7.2 16.3 %copy-start.34 = (s32[1,14,1024]{2,0,1:T(1,128)S(1)}, s32[1,14,1024]{2,0,1:T(1,128)}, u32[]{:S(2)}) copy-start(s32[1,14,1024]{2,0,1:T(1,128)} %param.21) | copy-start | bytes 172036
  10.2 71.1 %all-to-all-start.1 = ((f32[1,8,128,1,256]{4,1,3,0,2:T(8,128)}), f32[1,8,128,1,256]{4,1,3,0,2:T(8,128)S(1)}, u32[]{:S(2)}, u32[]{:S(2)}) async-start(f32[1,8,128,1,256]{4,1,3,0,2:T(8,128)} %copy.95), calls=%async_computation.1 | async-start | bytes 2097152 | tf_op jit(solution)/shard_map/all_to_all | solution.py:63
  28.1 4.6 copy-start.39
  28.1 4.6 copy-start.40
  28.1 4.6 copy-start.44
  32.7 12.5 %copy-start.12 = (f32[1,1024,256]{2,1,0:T(8,128)S(1)}, f32[1,1024,256]{2,1,0:T(8,128)}, u32[]{:S(2)}) copy-start(f32[1,1024,256]{2,1,0:T(8,128)} %param.19) | copy-start | bytes 3145732
  32.7 12.5 %copy-start.25 = (s32[256,1024]{0,1:T(8,128)S(1)}, s32[256,1024]{0,1:T(8,128)}, u32[]{:S(2)}) copy-start(s32[256,1024]{0,1:T(8,128)} %copy.92) | copy-start | bytes 3145732
  32.7 12.5 %copy-start.45 = (f32[1024,256]{1,0:T(8,128)S(1)}, f32[1024,256]{1,0:T(8,128)}, u32[]{:S(2)}) copy-start(f32[1024,256]{1,0:T(8,128)} %param.31) | copy-start | bytes 3145732
  45.2 6.0 copy-start.20
  45.2 6.0 copy-start.22
  51.2 5.0 copy-start.8
  51.2 6.0 copy-start.19
  55.6 1.0 copy-start.15
  56.2 14.7 %copy-start.10 = (f32[1,1024,256]{2,1,0:T(8,128)}, f32[1,1024,256]{2,1,0:T(8,128)S(1)}, u32[]{:S(2)}) copy-start(f32[1,1024,256]{2,1,0:T(8,128)S(1)} %get-tuple-element.27) | copy-start | bytes 3145732
  56.6 0.7 copy-start.35
  60.9 10.0 %copy-start.13 = (f32[1,1024,256]{2,1,0:T(8,128)S(1)}, f32[1,1024,256]{2,1,0:T(8,128)}, u32[]{:S(2)}) copy-start(f32[1,1024,256]{2,1,0:T(8,128)} %param.19) | copy-start | bytes 3145732
  60.9 10.0 %copy-start.21 = (f32[1024,1024]{1,0:T(8,128)S(1)}, f32[1024,1024]{1,0:T(8,128)}, u32[]{:S(2)}) copy-start(f32[1024,1024]{1,0:T(8,128)} %copy-done.20) | copy-start | bytes 12582916
  60.9 10.0 %copy-start.26 = (s32[256,1024]{0,1:T(8,128)S(1)}, s32[256,1024]{0,1:T(8,128)}, u32[]{:S(2)}) copy-start(s32[256,1024]{0,1:T(8,128)} %copy.92) | copy-start | bytes 3145732
  81.3 11.1 %copy-start.37 = (f32[256]{0:T(256)S(1)}, f32[256]{0:T(256)}, u32[]{:S(2)}) copy-start(f32[256]{0:T(256)} %param.23) | copy-start | bytes 3076
  81.3 11.1 %copy-start.43 = (f32[256]{0:T(256)S(1)}, f32[256]{0:T(256)}, u32[]{:S(2)}) copy-start(f32[256]{0:T(256)} %param.24) | copy-start | bytes 3076
  81.3 25.1 %copy-start.4 = (f32[1,8,128,1,256]{4,1,3,0,2:T(8,128)}, f32[1,8,128,1,256]{4,1,3,0,2:T(8,128)S(1)}, u32[]{:S(2)}) copy-start(f32[1,8,128,1,256]{4,1,3,0,2:T(8,128)S(1)} %all-to-all-done.1) | copy-start | bytes 3145732
  81.3 129.1 %all-to-all-start = ((f32[1,8,128,1,256]{4,1,3,0,2:T(8,128)}), f32[1,8,128,1,256]{4,1,3,0,2:T(8,128)S(1)}, u32[]{:S(2)}, u32[]{:S(2)}) async-start(f32[1,8,128,1,256]{4,1,3,0,2:T(8,128)} %copy.94), calls=%async_computation | async-start | bytes 2097152 | tf_op jit(solution)/shard_map/all_to_all | solution.py:63
  91.1 680.3 %all-reduce.7.cloned.1.call-start = ((), (), s32[]{:S(2)}) async-start(), calls=%async_computation.3 | async-start | bytes 6291456 | tf_op jit(solution)/shard_map/psum | solution.py:113
  91.4 1.0 copy-start.28
  92.7 13.7 %copy-start.17 = (f32[128,1,8,1,1,256]{5,2,0,4,3,1:T(8,128)}, f32[128,1,8,1,1,256]{5,2,0,4,3,1:T(8,128)S(1)}, u32[]{:S(2)}) copy-start(f32[128,1,8,1,1,256]{5,2,0,4,3,1:T(8,128)S(1)} %multiply_add_fusion.1) | copy-start | bytes 3145732
  195.3 15.1 %copy-start.32 = (f32[256,256]{1,0:T(8,128)S(1)}, f32[256,256]{1,0:T(8,128)}, u32[]{:S(2)}) copy-start(f32[256,256]{1,0:T(8,128)} %param.26) | copy-start | bytes 786436
  210.4 88.7 %copy-start.23 = (f32[1,8,128,1,256]{4,1,3,0,2:T(8,128)}, f32[1,8,128,1,256]{4,1,3,0,2:T(8,128)S(1)}, u32[]{:S(2)}) copy-start(f32[1,8,128,1,256]{4,1,3,0,2:T(8,128)S(1)} %all-to-all-done) | copy-start | bytes 3145732
  299.1 45.8 %copy-start.3 = (f32[8,16,8,8,32,1]{4,2,3,1,0,5:T(8,128)S(1)}, f32[8,16,8,8,32,1]{4,2,3,1,0,5:T(8,128)}, u32[]{:S(2)}) copy-start(f32[8,16,8,8,32,1]{4,2,3,1,0,5:T(8,128)} %get-tuple-element.31) | copy-start | bytes 3145732
  344.9 57.1 %copy-start.2 = (f32[16,8,32,8,8,1]{2,4,1,0,3,5:T(8,128)S(1)}, f32[16,8,32,8,8,1]{2,4,1,0,3,5:T(8,128)}, u32[]{:S(2)}) copy-start(f32[16,8,32,8,8,1]{2,4,1,0,3,5:T(8,128)} %convolution_bitcast_fusion.1) | copy-start | bytes 3145732
  402.0 51.1 %copy-start.6 = (f32[8,16,8,8,32,1]{4,2,3,1,0,5:T(8,128)S(1)}, f32[8,16,8,8,32,1]{4,2,3,1,0,5:T(8,128)}, u32[]{:S(2)}) copy-start(f32[8,16,8,8,32,1]{4,2,3,1,0,5:T(8,128)} %get-tuple-element.30) | copy-start | bytes 3145732
  584.7 9.9 %copy-start.18 = (f32[128,1,8,1,1,256]{5,2,0,4,3,1:T(8,128)S(1)}, f32[128,1,8,1,1,256]{5,2,0,4,3,1:T(8,128)}, u32[]{:S(2)}) copy-start(f32[128,1,8,1,1,256]{5,2,0,4,3,1:T(8,128)} %copy-done.17) | copy-start | bytes 3145732
  594.6 5.8 copy-start.5
  594.6 5.8 copy-start.9
  594.6 5.8 copy-start.27
  594.6 5.8 copy-start.29
  594.6 5.8 copy-start.38
  600.4 2.9 copy-start.31
  600.4 4.5 copy-start.24
  603.2 1.0 copy-start.16
  607.4 13.9 %copy-start.42 = (f32[1024]{0:T(1024)S(1)}, f32[1024]{0:T(1024)}, u32[]{:S(2)}) copy-start(f32[1024]{0:T(1024)} %get-tuple-element.47) | copy-start | bytes 12292
  607.4 13.9 %copy-start.41 = (f32[256]{0:T(256)S(1)}, f32[256]{0:T(256)}, u32[]{:S(2)}) copy-start(f32[256]{0:T(256)} %get-tuple-element.13) | copy-start | bytes 3076
  607.4 85.5 %copy-start.11 = (f32[1,1024,256]{2,1,0:T(8,128)S(1)}, f32[1,1024,256]{2,1,0:T(8,128)}, u32[]{:S(2)}) copy-start(f32[1,1024,256]{2,1,0:T(8,128)} %copy-done.10) | copy-start | bytes 3145732
  607.4 85.5 %copy-start.14 = (f32[1,1024,256]{2,1,0:T(8,128)S(1)}, f32[1,1024,256]{2,1,0:T(8,128)}, u32[]{:S(2)}) copy-start(f32[1,1024,256]{2,1,0:T(8,128)} %param.19) | copy-start | bytes 3145732
  607.5 85.5 %copy-start.36 = (f32[1024]{0:T(1024)S(1)}, f32[1024]{0:T(1024)}, u32[]{:S(2)}) copy-start(f32[1024]{0:T(1024)} %copy-done.35) | copy-start | bytes 12292
  610.1 82.5 %all-to-all-start.2 = ((f32[128,8,1,1,256]{4,1,3,2,0:T(8,128)}), f32[128,8,1,1,256]{4,1,3,2,0:T(8,128)S(1)}, u32[]{:S(2)}, u32[]{:S(2)}) async-start(f32[128,8,1,1,256]{4,1,3,2,0:T(8,128)} %bitcast.248), calls=%async_computation.2 | async-start | bytes 2097152 | tf_op jit(solution)/shard_map/all_to_all | solution.py:71
  693.0 85.5 %copy-start.1 = (f32[256,1024]{1,0:T(8,128)S(1)}, f32[256,1024]{1,0:T(8,128)}, u32[]{:S(2)}) copy-start(f32[256,1024]{1,0:T(8,128)} %param.29) | copy-start | bytes 3145732
  771.4 6.1 copy-start.30
Sparse Core Ops, SparseCore 0:
  607.6 163.7 all-reduce.6
where the time goes:
time: 796 us; the launch traced here: 786 us
  matrix products  434 us (55%)
  other arithmetic  84 us (11%)
  waiting for transfers between devices  77.2 us (10%)
  local copies, waits for them, and re-layouts  73.5 us (9%)
  blocking collectives  71.3 us (9%)
  starting transfers between devices  31.1 us (4%)
  between operations  15.1 us (2%)
    dot_general x3, matrix products, attend(): jnp.einsum('abnijkl,' + key_layout + '->' + layout, weights, values_in, p...  192 us
    dot_general x3, matrix products, attend(): jnp.einsum(layout + ',' + key_layout + '->abnijkl', queries, keys_in, pre...  172 us
    psum x1, waiting for transfers between devices, local(): lax.psum((attn_grads[1] * grad_scale, attn_grads[2] * grad_scale, attn_gr...  77.1 us
    psum x1, blocking collectives, local(): lax.psum((attn_grads[1] * grad_scale, attn_grads[2] * grad_scale, attn_gr...  71.3 us
    div x2, other arithmetic, attend(): jax.nn.softmax(scores.reshape(score_shape[:5] + (-1,)), axis=-1)  45.8 us
    dot_general x3, matrix products, ffn_branch(): jnp.einsum('...c,cf->...f', normed, w_up, precision=PRECISE) + up_bias  23.9 us
    another operation x3, local copies, waits for them, and re-layouts  23.3 us
    dot_general x3, matrix products, attention_branch(): projected = jnp.einsum('...c,ce->...e', normed, w_qkv, precision=PRECISE)  22.2 us
  transfers between devices with their start and end apart: 4, of which 1 were waited for; matrix products, arithmetic and copies ran while one was open for 23% of the time, Pallas kernels for 0%

commit v1 on v0

v1 whole, which is shorter than its diff:
```python
from functools import partial

import jax
import jax.numpy as jnp
from jax import lax
from jax.experimental import pallas as pl
from jax.experimental.pallas import tpu as pltpu
from jax.sharding import PartitionSpec as P

NH = 8
HD = 32
D = 256
FF = 1024
EPSILON = 1e-05
KEEP_SCALE = 8.0 / 3.0
BITS = 19
BF = jnp.bfloat16
F32 = jnp.float32

NN = (((1,), (0,)), ((), ()))
NT = (((1,), (1,)), ((), ()))
TN = (((0,), (0,)), ((), ()))


def mm(a, b, dims):
    return lax.dot_general(a, b, dims, preferred_element_type=F32)


def split(x):
    high = x.astype(BF)
    return high, (x - high.astype(F32)).astype(BF)


def cat(parts, axis):
    return jnp.concatenate(parts, axis=axis)


def norm_stats(x):
    average = jnp.mean(x, -1, keepdims=True)
    centred = x - average
    spread = jnp.mean(centred * centred, -1, keepdims=True)
    inverse = lax.rsqrt(spread + EPSILON)
    return centred * inverse, inverse


def norm_back(d_normed, unit, inverse, gain):
    d_unit = d_normed * gain
    return inverse * (
        d_unit
        - jnp.mean(d_unit, -1, keepdims=True)
        - unit * jnp.mean(d_unit * unit, -1, keepdims=True)
    )


def keep_factor(words, flag, selector):
    kept = words * flag
    bits = cat([(lax.shift_right_logical(kept, s) & 1).astype(F32) for s in range(BITS)], 0)
    return mm(bits.astype(BF), selector, TN) * KEEP_SCALE


def make_selector():
    line = lax.broadcasted_iota(jnp.int32, (16 * BITS, D), 0)
    channel = lax.broadcasted_iota(jnp.int32, (16 * BITS, D), 1)
    return (channel == (line & 15) * BITS + (line >> 4)).astype(F32).astype(BF)


ROOT_HALF = 0.7071067811865476
DENSITY = 0.3989422804014327


def ffn_prepare(w_up, up_bias, w_down, up3, upt3, down3, bias_t):
    for f in range(4):
        block = w_up[:, 256 * f : 256 * f + 256]
        high, low = split(block)
        up3[f] = cat([high, low, high], 1)
        high, low = split(jnp.transpose(block))
        upt3[256 * f : 256 * f + 256, :] = cat([high, low, high], 1)
        high, low = split(w_down[256 * f : 256 * f + 256, :])
        down3[256 * f : 256 * f + 256, :] = cat([high, low, high], 1)
        bias = jnp.broadcast_to(up_bias[:, 256 * f : 256 * f + 256], (256, 256))
        bias_t[256 * f : 256 * f + 256, :] = jnp.transpose(bias)


def ffn_chunk(x, up, factor, gain, shift, up3, upt3, down3, bias_t, d_up_t, d_down, d_bias, first):
    unit, inverse = norm_stats(x)
    normed = unit * gain + shift
    grad = up * factor
    nh, nl = split(normed)
    gh, gl = split(grad)
    n_lanes, g_lanes = cat([nh, nh, nl], 1), cat([gh, gh, gl], 1)
    n_rows, g_rows = cat([nh, nh, nl], 0), cat([gh, gh, gl], 0)
    dn_t = None
    for f in range(4):
        rows = slice(256 * f, 256 * f + 256)
        pre = mm(upt3[rows, :], n_lanes, NT) + bias_t[rows, :]
        d_hidden = mm(down3[rows, :], g_lanes, NT)
        cdf = 0.5 * (1.0 + lax.erf(pre * ROOT_HALF))
        density = DENSITY * jnp.exp(-0.5 * pre * pre)
        hidden = pre * cdf
        d_pre = d_hidden * (cdf + pre * density)
        hh, hl = split(hidden)
        ph, pw = split(d_pre)
        part = mm(up3[f], cat([ph, ph, pw], 0), NN)
        dn_t = part if dn_t is None else dn_t + part
        down_part = mm(cat([hh, hl, hh], 1), g_rows, NN)
        up_part = mm(cat([ph, pw, ph], 1), n_rows, NN)
        bias_part = d_pre[:, :128] + d_pre[:, 128:]
        if first is True:
            d_down[rows, :] = down_part
            d_up_t[rows, :] = up_part
            d_bias[rows, :] = bias_part
        else:
            d_down[rows, :] += down_part
            d_up_t[rows, :] += up_part
            d_bias[rows, :] += bias_part
    d_normed = jnp.transpose(dn_t)
    d_x = norm_back(d_normed, unit, inverse, gain)
    return d_x, d_normed * unit, d_normed


def fold_rows(x):
    rows = x.shape[0]
    return jnp.sum(x.reshape(rows // 8, 8, x.shape[1]), axis=0)


def head_mask(rows, head):
    lane = lax.broadcasted_iota(jnp.int32, (rows, D), 1)
    return (lane >> 5) == head


def spread_heads(x):
    zero = jnp.zeros_like(x)
    return cat([jnp.where(head_mask(64, h), x, zero) for h in range(NH)], 0)


def pick_heads(full):
    out = full[0:64]
    for h in range(1, NH):
        out = jnp.where(head_mask(64, h), full[64 * h : 64 * h + 64], out)
    return out


def group_core(q, k, v, g):
    qh, ql = split(q)
    kh, kl = split(k)
    vh, vl = split(v)
    gh, gl = split(g)
    q_high, q_low = spread_heads(qh), spread_heads(ql)
    g_high, g_low = spread_heads(gh), spread_heads(gl)
    two = mm(cat([kh, kl], 0), q_high, NT)
    scores = two[:64] + two[64:] + mm(kh, q_low, NT)
    scores = jnp.exp(scores - jnp.max(scores, axis=0, keepdims=True))
    p = scores * (1.0 / jnp.sum(scores, axis=0, keepdims=True))
    two = mm(cat([vh, vl], 0), g_high, NT)
    dp = two[:64] + two[64:] + mm(vh, g_low, NT)
    ds = p * (dp - jnp.sum(p * dp, axis=0, keepdims=True))
    ph, pw = split(p)
    sh, sw = split(ds)
    two = mm(cat([ph, pw], 0), g_high, NN)
    dv = two[:64] + two[64:] + mm(ph, g_low, NN)
    two = mm(cat([sh, sw], 0), q_high, NN)
    dk = two[:64] + two[64:] + mm(sh, q_low, NN)
    mixed = pick_heads(mm(cat([ph, pw, ph], 0), cat([vh, vh, vl], 0), TN))
    dq = pick_heads(mm(cat([sh, sw, sh], 0), cat([kh, kh, kl], 0), TN))
    return mixed, dq, dk, dv


def get(ref, part, rows):
    return cat([ref[2 * part, rows, :], ref[2 * part + 1, rows, :]], 1)


def put(ref, part, rows, x):
    ref[2 * part, rows, :] = x[:, :128]
    ref[2 * part + 1, rows, :] = x[:, 128:]

MESH = pl.DeviceIdType.MESH
MID_GROUP = 10


def remote(src, dst, send, recv, device):
    return pltpu.make_async_remote_copy(
        src_ref=src, dst_ref=dst, send_sem=send, recv_sem=recv, device_id=(device,), device_id_type=MESH
    )


def arrived(ref, sem):
    pltpu.make_async_copy(ref, ref, sem).wait()


def kernel(tokens, stored, upstream, drop_attn, drop_ffn, depth_keep, gain_one, shift_one, w_qkv, w_out,
           gain_two, shift_two, w_up, up_bias, w_down,
           result, out_gain_one, out_shift_one, out_qkv, out_out, out_gain_two, out_shift_two, out_up, out_bias, out_down,
           up3, upt3, down3, bias_t, d_bias, factor_ffn, factor_attn, through, branch,
           grid_tokens, grid_grad, d_grid, back,
           ffn_sum, ffn_half, ffn_slots, ffn_mine, ffn_all,
           att_sum, att_half, att_slots, att_mine, att_all,
           vec_two, vec_two_slots, vec_one, vec_one_slots, vec_core, vec_pair,
           qkv, mixed, d_qkv, d_mixed, unit_s, inverse_s, normed_t,
           send, recv, local):
    me = lax.axis_index("rows")
    spot, core = me // 2, me % 2
    pair = me + 1 - 2 * core
    band, lane = me // 16, me % 16
    grad_scale = float(1024 * 128) ** (-0.5)

    def same_core(k):
        return ((spot + k) % 64) * 2 + core

    barrier = pltpu.get_barrier_semaphore()

    @pl.loop(1, 64)
    def _(k):
        pl.semaphore_signal(barrier, inc=1, device_id=(same_core(k),), device_id_type=MESH)

    pl.semaphore_signal(barrier, inc=1, device_id=(pair,), device_id_type=MESH)

    ffn_prepare(w_up, up_bias, w_down, up3, upt3, down3, bias_t)
    selector = make_selector()
    zeros = jnp.zeros((2, 1024), jnp.int32)
    tile = lax.broadcasted_iota(jnp.int32, (128, 1024), 0)
    column = lax.broadcasted_iota(jnp.int32, (128, 1024), 1)
    widen = (tile == (column >> 3)).astype(F32).astype(BF)
    flags = [
        mm(jnp.broadcast_to(depth_keep[n, pl.ds(me // 8, 1), :].astype(F32), (8, 128)).astype(BF), widen, NN)[0:1].astype(jnp.int32)
        for n in range(2)
    ]
    for n, (words, factor) in enumerate(((drop_attn, factor_attn), (drop_ffn, factor_ffn))):
        kept = keep_factor(cat([words[...], zeros], 0), flags[n], selector)
        factor[...] = kept.reshape(8, 128, D)

    pl.semaphore_wait(barrier, 64)

    def token_piece(who):
        return tokens.at[:, pl.ds(pl.multiple_of(16 * who, 16), 16), :]

    def branch_piece(who):
        return branch.at[:, pl.ds(pl.multiple_of(16 * who, 16), 16), :]

    own_tokens = pltpu.make_async_copy(token_piece(band), grid_tokens.at[band], recv.at[0])
    own_tokens.start()

    @pl.loop(1, 8)
    def _(k):
        who = (band + k) % 8
        remote(token_piece(who), grid_tokens.at[band], send.at[0], recv.at[0], who * 16 + lane).start()

    ffn_sum[...] = jnp.zeros_like(ffn_sum)
    d_bias[...] = jnp.zeros_like(d_bias)
    vec_two[...] = jnp.zeros_like(vec_two)
    d_up_t, d_down = ffn_sum.at[0:1024], ffn_sum.at[1024:2048]

    def send_branch(who):
        remote(branch_piece(who), grid_grad.at[band], send.at[1], recv.at[1], who * 16 + lane).start()

    @pl.loop(0, 4)
    def _(s):
        offset = 2 - s + 3 * (s // 2) - 2 * (s // 3)
        q = (band // 2 + offset) % 4
        cols = pl.ds(pl.multiple_of(q * 32, 32), 32)
        up = upstream[:, cols, :].reshape(256, D)
        d_x, d_gain, d_shift = ffn_chunk(
            stored[:, cols, :].reshape(256, D), up, factor_ffn[:, cols, :].reshape(256, D),
            gain_two[...], shift_two[...], up3, upt3, down3, bias_t, d_up_t, d_down, d_bias, False)
        total = up + d_x
        through[:, cols, :] = total.reshape(8, 32, D)
        branch[:, cols, :] = (total * factor_attn[:, cols, :].reshape(256, D)).reshape(8, 32, D)
        vec_two[0:1, :] += jnp.sum(d_gain, axis=0, keepdims=True)
        vec_two[1:2, :] += jnp.sum(d_shift, axis=0, keepdims=True)

        @pl.when(s < 3)
        def _():
            send_branch(2 * q)
            send_branch(2 * q + 1)

        @pl.when(s == 3)
        def _():
            send_branch(band + 1 - 2 * (band % 2))
            pltpu.make_async_copy(branch_piece(band), grid_grad.at[band], recv.at[1]).start()

    for f in range(4):
        vec_two[2 + f : 3 + f, :] = jnp.sum(jnp.transpose(d_bias[256 * f : 256 * f + 256, :]), axis=0, keepdims=True)

    ffn_pair = remote(
        ffn_sum.at[pl.ds(pl.multiple_of((1 - core) * 1024, 1024), 1024)], ffn_half, send.at[2], recv.at[2], pair)
    ffn_pair.start()
    own_vec_two = pltpu.make_async_copy(vec_two, vec_two_slots.at[spot], recv.at[3])
    own_vec_two.start()

    @pl.loop(1, 64)
    def _(k):
        remote(vec_two, vec_two_slots.at[spot], send.at[3], recv.at[3], same_core(k)).start()

    scale = HD ** (-0.5)
    wh, wl = split(w_qkv[...])
    w_rows = cat([wh, wh, wl], 0)
    arrived(grid_tokens, recv.at[0])
    for c in range(4):
        rows = slice(256 * c, 256 * c + 256)
        unit, inverse = norm_stats(grid_tokens[2 * c : 2 * c + 2].reshape(256, D))
        unit_s[rows, :] = unit
        inverse_s[rows, :] = jnp.broadcast_to(inverse, (256, 128))
        normed = unit * gain_one[...] + shift_one[...]
        normed_t[:, rows] = jnp.transpose(normed)
        nh, nl = split(normed)
        out = mm(cat([nh, nl, nh], 1), w_rows, NN)
        put(qkv, 0, rows, out[:, :256] * scale)
        put(qkv, 1, rows, out[:, 256:512])
        put(qkv, 2, rows, out[:, 512:])

    ffn_pair.wait()
    ffn_half[...] += ffn_sum[pl.ds(pl.multiple_of(core * 1024, 1024), 1024), :]

    @pl.loop(1, 64)
    def _(k):
        rows = pl.ds(pl.multiple_of(((spot + k) % 64) * 16, 16), 16)
        remote(ffn_half.at[rows], ffn_slots.at[k - 1], send.at[4], recv.at[4], same_core(k)).start()

    oh, ol = split(w_out[...])
    o_lanes = cat([oh, oh, ol], 1)
    arrived(grid_grad, recv.at[1])
    for c in range(4):
        rows = slice(256 * c, 256 * c + 256)
        gh, gl = split(grid_grad[2 * c : 2 * c + 2].reshape(256, D))
        put(d_mixed, 0, rows, mm(cat([gh, gl, gh], 1), o_lanes, NT))

    def ffn_gather(k):
        rows = pl.ds(pl.multiple_of(core * 1024 + spot * 16, 16), 16)
        return ffn_all.at[rows]

    @pl.loop(0, 16)
    def _(b):
        own = pl.ds(b, 64, stride=16)
        m, dq, dk, dv = group_core(get(qkv, 0, own), get(qkv, 1, own), get(qkv, 2, own), get(d_mixed, 0, own))
        put(mixed, 0, own, m)
        put(d_qkv, 0, own, dq * scale)
        put(d_qkv, 1, own, dk)
        put(d_qkv, 2, own, dv)

        @pl.when(b == MID_GROUP)
        def _():
            arrived(ffn_slots, recv.at[4])
            mine = ffn_half[pl.ds(pl.multiple_of(spot * 16, 16), 16), :]
            ffn_mine[...] = (mine + jnp.sum(ffn_slots[...], axis=0)) * grad_scale
            pltpu.make_async_copy(ffn_mine, ffn_gather(0), recv.at[5]).start()

            @pl.loop(1, 64)
            def _(k):
                remote(ffn_mine, ffn_gather(k), send.at[5], recv.at[5], same_core(k)).start()

    w_lanes = cat([wh, wh, wl], 1)
    d_gain = jnp.zeros((8, D), F32)
    d_shift = jnp.zeros((8, D), F32)

    def back_piece(who):
        return back.at[:, pl.ds(pl.multiple_of(16 * who, 16), 16), :]

    for c in range(4):
        rows = slice(256 * c, 256 * c + 256)
        dh, dl = split(cat([d_qkv[i, rows, :] for i in range(6)], 1))
        dn = mm(cat([dh, dl, dh], 1), w_lanes, NT)
        unit = unit_s[rows, :]
        inverse = inverse_s[rows, 0:1]
        d_grid[2 * c : 2 * c + 2] = norm_back(dn, unit, inverse, gain_one[...]).reshape(2, 8, 16, D)
        d_gain += fold_rows(dn * unit)
        d_shift += fold_rows(dn)

    pltpu.make_async_copy(d_grid.at[band], back_piece(band), recv.at[6]).start()

    @pl.loop(1, 8)
    def _(k):
        who = (band + k) % 8
        remote(d_grid.at[who], back_piece(band), send.at[6], recv.at[6], who * 16 + lane).start()

    vec_one[0:1, :] = jnp.sum(d_gain, axis=0, keepdims=True)
    vec_one[1:2, :] = jnp.sum(d_shift, axis=0, keepdims=True)
    pltpu.make_async_copy(vec_one, vec_one_slots.at[spot], recv.at[7]).start()

    @pl.loop(1, 64)
    def _(k):
        remote(vec_one, vec_one_slots.at[spot], send.at[7], recv.at[7], same_core(k)).start()

    for c in range(4):
        rows = slice(256 * c, 256 * c + 256)
        dh, dl = split(cat([d_qkv[i, rows, :] for i in range(6)], 1))
        nh, nl = split(normed_t[:, rows])
        part = mm(cat([nh, nl, nh], 1), cat([dh, dh, dl], 0), NN)
        mh, ml = split(jnp.transpose(get(mixed, 0, rows)))
        gh, gl = split(grid_grad[2 * c : 2 * c + 2].reshape(256, D))
        part_o = mm(cat([mh, ml, mh], 1), cat([gh, gh, gl], 0), NN)
        for n in range(4):
            piece = part_o if n == 3 else part[:, 256 * n : 256 * n + 256]
            if c == 0:
                att_sum[256 * n : 256 * n + 256, :] = piece
            else:
                att_sum[256 * n : 256 * n + 256, :] += piece

    att_pair = remote(
        att_sum.at[pl.ds(pl.multiple_of((1 - core) * 512, 512), 512)], att_half, send.at[8], recv.at[8], pair)
    att_pair.start()

    arrived(ffn_all.at[pl.ds(pl.multiple_of(core * 1024, 1024), 1024)], recv.at[5])
    ffn_rows = ffn_all.at[pl.ds(pl.multiple_of(core * 1024, 1024), 1024)]
    ffn_swap = remote(ffn_rows, ffn_rows, send.at[9], recv.at[9], pair)
    ffn_swap.start()

    att_pair.wait()
    att_half[...] += att_sum[pl.ds(pl.multiple_of(core * 512, 512), 512), :]

    @pl.loop(1, 64)
    def _(k):
        rows = pl.ds(pl.multiple_of(((spot + k) % 64) * 8, 8), 8)
        remote(att_half.at[rows], att_slots.at[k - 1], send.at[10], recv.at[10], same_core(k)).start()

    arrived(vec_two_slots, recv.at[3])
    arrived(vec_one_slots, recv.at[7])
    vec_core[0:8, :] = jnp.sum(vec_two_slots[...], axis=0)
    vec_core[8:10, :] = jnp.sum(vec_one_slots[...], axis=0)
    vec_core[10:16, :] = jnp.zeros((6, D), F32)
    vec_swap = remote(vec_core, vec_pair, send.at[11], recv.at[11], pair)
    vec_swap.start()

    arrived(back, recv.at[6])
    result[...] = through[...] + back[...]
    vec_swap.wait()
    total = (vec_core[...] + vec_pair[...]) * grad_scale
    out_gain_two[...] = total[0:1]
    out_shift_two[...] = total[1:2]
    for f in range(4):
        out_bias[:, 256 * f : 256 * f + 256] = total[2 + f : 3 + f]
    out_gain_one[...] = total[8:9]
    out_shift_one[...] = total[9:10]

    arrived(att_slots, recv.at[10])
    mine = att_half[pl.ds(pl.multiple_of(spot * 8, 8), 8), :]
    att_mine[...] = (mine + jnp.sum(att_slots[...], axis=0)) * grad_scale
    att_spot = att_all.at[pl.ds(pl.multiple_of(core * 512 + spot * 8, 8), 8)]
    pltpu.make_async_copy(att_mine, att_spot, recv.at[12]).start()

    @pl.loop(1, 64)
    def _(k):
        remote(att_mine, att_spot, send.at[12], recv.at[12], same_core(k)).start()

    ffn_swap.wait()
    for f in range(4):
        rows = slice(256 * f, 256 * f + 256)
        out_up[:, rows] = jnp.transpose(ffn_all[rows, :])
        out_down[rows, :] = ffn_all[1024 + 256 * f : 1280 + 256 * f, :]

    att_rows = att_all.at[pl.ds(pl.multiple_of(core * 512, 512), 512)]
    arrived(att_rows, recv.at[12])
    att_swap = remote(att_rows, att_rows, send.at[13], recv.at[13], pair)
    att_swap.start()
    arrived(grid_tokens.at[0:7], send.at[0])
    arrived(grid_grad.at[0:7], send.at[1])
    arrived(vec_two_slots.at[0:63], send.at[3])
    arrived(ffn_slots, send.at[4])
    arrived(ffn_slots, send.at[5])
    arrived(d_grid.at[0:7], send.at[6])
    arrived(vec_one_slots.at[0:63], send.at[7])
    arrived(att_slots, send.at[10])
    arrived(att_slots, send.at[12])
    att_swap.wait()
    for n in range(3):
        out_qkv[:, 256 * n : 256 * n + 256] = att_all[256 * n : 256 * n + 256, :]
    out_out[...] = att_all[768:1024, :]


VM = pl.BlockSpec(memory_space=pltpu.VMEM)
HB = pl.BlockSpec(memory_space=pl.ANY)
LIMIT = 62 * 1024 * 1024


def shape(*dims):
    return jax.ShapeDtypeStruct(dims, F32)


def local(tokens, stored, upstream, drop_attn, drop_ffn, depth_keep, gain_one, shift_one, w_qkv, w_out,
          gain_two, shift_two, w_up, up_bias, w_down):
    def v(*dims):
        return pltpu.VMEM(dims, F32)

    outs = pl.pallas_call(
        kernel,
        out_shape=(shape(8, 128, D), shape(1, D), shape(1, D), shape(D, 768), shape(D, D), shape(1, D), shape(1, D),
                   shape(D, FF), shape(1, FF), shape(FF, D)),
        in_specs=[HB] + [VM] * 14,
        out_specs=(VM,) * 10,
        scratch_shapes=[
            pltpu.VMEM((4, 256, 768), BF), pltpu.VMEM((1024, 768), BF), pltpu.VMEM((1024, 768), BF),
            v(1024, 256), v(1024, 128), v(8, 128, D), v(8, 128, D), v(8, 128, D), v(8, 128, D),
            v(8, 8, 16, D), v(8, 8, 16, D), v(8, 8, 16, D), v(8, 128, D),
            v(2048, D), v(1024, D), v(63, 16, D), v(16, D), v(2048, D),
            v(1024, D), v(512, D), v(63, 8, D), v(8, D), v(1024, D),
            v(8, D), v(64, 8, D), v(2, D), v(64, 2, D), v(16, D), v(16, D),
            v(6, 1024, 128), v(2, 1024, 128), v(6, 1024, 128), v(2, 1024, 128), v(1024, 256), v(1024, 128), v(256, 1024),
            pltpu.SemaphoreType.DMA((14,)), pltpu.SemaphoreType.DMA((14,)), pltpu.SemaphoreType.DMA((1,))],
        compiler_params=pltpu.CompilerParams(vmem_limit_bytes=LIMIT, collective_id=0, has_side_effects=True),
        name="block_back",
    )(tokens.reshape(8, 128, D), stored.reshape(8, 128, D), upstream.reshape(8, 128, D), drop_attn[0], drop_ffn[0], depth_keep,
      gain_one[None], shift_one[None], w_qkv, w_out, gain_two[None], shift_two[None], w_up, up_bias[None], w_down)
    result, gain_one, shift_one, d_qkv, d_out, gain_two, shift_two, d_up, bias, d_down = outs
    return (result.reshape(1, 1024, D), gain_one[0], shift_one[0], d_qkv, d_out, gain_two[0], shift_two[0], d_up, bias[0], d_down)


def solution(mesh):
    banded = P("rows", None, None)
    return jax.shard_map(
        local,
        mesh=mesh,
        in_specs=(banded,) * 5 + (P(),) * 10,
        out_specs=(banded,) + (P(),) * 9,
        check_vma=False,
    )
```

time: 796 us -> 121 us (0.15); the launches traced: 786 us -> 121 us
  matrix products: 434 us -> 0 us
  Pallas kernels: 0 us -> 110 us
  other arithmetic: 84 us -> 0 us
  waiting for transfers between devices: 77.2 us -> 0 us
  blocking collectives: 71.3 us -> 0 us
  local copies, waits for them, and re-layouts: 73.5 us -> 10.7 us
  starting transfers between devices: 31.1 us -> 0 us
  between operations: 15.1 us -> 0.68 us
    dot_general x16 -> x0, matrix products: 434 us -> none  [the longest x3 192 us: attend(): jnp.einsum('abnijkl,' + key_layout + '->' + layout, weights, values_in, p...]
    pallas_call x0 -> x1, Pallas kernels: none -> 110 us  [local(): pl.pallas_call(kernel, out_shape=(shape(8, 128, D), shape(1, D), shape(1,...]
    psum x1 -> x0, waiting for transfers between devices: 77.1 us -> none  [local(): lax.psum((attn_grads[1] * grad_scale, attn_grads[2] * grad_scale, attn_gr...]
    psum x1 -> x0, blocking collectives: 71.3 us -> none  [local(): lax.psum((attn_grads[1] * grad_scale, attn_grads[2] * grad_scale, attn_gr...]
    div x8 -> x0, other arithmetic: 45.9 us -> none  [the longest x2 45.8 us: attend(): jax.nn.softmax(scores.reshape(score_shape[:5] + (-1,)), axis=-1)]
    all_to_all x3 -> x0, starting transfers between devices: 31 us -> none  [the longest x2 21.3 us: direct_out(): lax.all_to_all(shaped, 'rows', split_axis=2, concat_axis=0, tiled=True)]
    another operation x3 -> x0, local copies, waits for them, and re-layouts: 23.3 us -> none
    reduce_sum x8 -> x0, other arithmetic: 18.8 us -> none  [the longest x1 15 us: attend(): jax.nn.softmax(scores.reshape(score_shape[:5] + (-1,)), axis=-1)]
  transfers between devices with their start and end apart: 4 -> 0, of which waited for: 1 -> 0; matrix products, arithmetic and copies ran while one was open for 23% -> 0% of each run, Pallas kernels for 0% -> 0%
where the time goes in v1:
time: 121 us
  Pallas kernels  110 us (91%)
  local copies, waits for them, and re-layouts  10.7 us (9%)
    pallas_call x1, Pallas kernels, local(): pl.pallas_call(kernel, out_shape=(shape(8, 128, D), shape(1, D), shape(1,...  110 us
    unnamed x29, local copies, waits for them, and re-layouts  10.7 us

profile of v1, /device:TPU:1, one launch (start us, length us, event | category | flops | bytes accessed | tf_op | source)
XLA Modules:
  0.0 121.1 jit_solution(6793819248062225346)
XLA Ops:
  0.6 1.5 %copy_bitcast_fusion = (s32[14,1024]{1,0:T(8,128)}, s32[14,1024]{1,0:T(8,128)}) fusion(s32[1,14,1024]{2,0,1:T(1,128)} %param.19, s32[1,14,1024]{2,0,1:T(1,128)} %param.18), kind=kLoop, calls=%fused_computation | loop fusion | bytes 229376
  2.2 109.7 %block_back.1 = (f32[8,128,256]{2,1,0:T(8,128)}, f32[1,256]{1,0:T(1,128)}, f32[1,256]{1,0:T(1,128)}, f32[256,768]{1,0:T(8,128)}, f32[256,256]{1,0:T(8,128)}, /*i...) custom-call(f32[8,128,256]{2,1,0:T(8,128)} %bitcast.18, ...), custom_call_target="tpu_custom_call" | custom-call | tf_op jit(solution)/shard_map/block_back/pallas_call | solution.py:482
  111.9 0.0 copy-start.8
  111.9 0.0 copy-start.2
  111.9 2.3 %copy.39 = f32[1,1024,256]{2,1,0:T(8,128)} copy(f32[1,1024,256]{2,1,0:T(8,128)} %bitcast.21) | data formatting | bytes 2097152
  114.2 0.0 copy-done.8
  114.2 0.0 copy-start.7
  114.3 0.6 copy.40
  114.8 0.1 copy-done.7
  114.9 0.6 copy.41
  115.5 0.0 copy-done.2
  115.5 0.0 copy-start.3
  115.5 0.0 copy-start.1
  115.5 0.9 copy.42
  116.4 0.2 copy-done.3
  116.6 0.0 copy-start.6
  116.6 0.7 copy.43
  117.3 0.0 copy-done.6
  117.3 0.0 copy-start.5
  117.3 0.6 copy.44
  117.9 0.1 copy-done.5
  118.0 0.6 copy.45
  118.5 0.0 copy-done.1
  118.5 0.0 copy-start.4
  118.5 0.0 copy-start
  118.5 1.0 copy.46
  119.5 0.0 copy-done.4
  119.5 0.6 copy.47
  120.1 0.0 copy-done
  120.1 1.0 copy.48
Async XLA Ops:
  111.9 2.4 %copy-start.8 = (f32[1,256]{1,0:T(1,128)S(1)}, f32[1,256]{1,0:T(1,128)}, u32[]{:S(2)}) copy-start(f32[1,256]{1,0:T(1,128)} %get-tuple-element.21) | copy-start | bytes 3076
  111.9 3.6 %copy-start.2 = (f32[256,768]{1,0:T(8,128)S(1)}, f32[256,768]{1,0:T(8,128)}, u32[]{:S(2)}) copy-start(f32[256,768]{1,0:T(8,128)} %get-tuple-element.45) | copy-start | bytes 2359300
  114.2 0.7 copy-start.7
  115.5 1.1 copy-start.3
  115.5 3.0 %copy-start.1 = (f32[256,1024]{1,0:T(8,128)S(1)}, f32[256,1024]{1,0:T(8,128)}, u32[]{:S(2)}) copy-start(f32[256,1024]{1,0:T(8,128)} %get-tuple-element.49) | copy-start | bytes 3145732
  116.6 0.7 copy-start.6
  117.3 0.7 copy-start.5
  118.5 1.0 copy-start.4
  118.5 1.6 %copy-start = (f32[1024,256]{1,0:T(8,128)S(1)}, f32[1024,256]{1,0:T(8,128)}, u32[]{:S(2)}) copy-start(f32[1024,256]{1,0:T(8,128)} %get-tuple-element.51) | copy-start | bytes 3145732

commit v2 on v1

v2 whole, which is shorter than its diff:
```python
from functools import partial

import jax
import jax.numpy as jnp
from jax import lax
from jax.experimental import pallas as pl
from jax.experimental.pallas import tpu as pltpu
from jax.sharding import PartitionSpec as P

NH = 8
HD = 32
D = 256
FF = 1024
EPSILON = 1e-05
KEEP_SCALE = 8.0 / 3.0
BITS = 19
BF = jnp.bfloat16
F32 = jnp.float32

NN = (((1,), (0,)), ((), ()))
NT = (((1,), (1,)), ((), ()))
TN = (((0,), (0,)), ((), ()))


def mm(a, b, dims):
    return lax.dot_general(a, b, dims, preferred_element_type=F32)


def split(x):
    high = x.astype(BF)
    return high, (x - high.astype(F32)).astype(BF)


def cat(parts, axis):
    return jnp.concatenate(parts, axis=axis)


def norm_stats(x):
    average = jnp.mean(x, -1, keepdims=True)
    centred = x - average
    spread = jnp.mean(centred * centred, -1, keepdims=True)
    inverse = lax.rsqrt(spread + EPSILON)
    return centred * inverse, inverse


def norm_back(d_normed, unit, inverse, gain):
    d_unit = d_normed * gain
    return inverse * (
        d_unit
        - jnp.mean(d_unit, -1, keepdims=True)
        - unit * jnp.mean(d_unit * unit, -1, keepdims=True)
    )


def keep_factor(words, flag, selector):
    kept = words * flag
    bits = cat([(lax.shift_right_logical(kept, s) & 1).astype(F32) for s in range(BITS)], 0)
    return mm(bits.astype(BF), selector, TN) * KEEP_SCALE


def make_selector():
    line = lax.broadcasted_iota(jnp.int32, (16 * BITS, D), 0)
    channel = lax.broadcasted_iota(jnp.int32, (16 * BITS, D), 1)
    return (channel == (line & 15) * BITS + (line >> 4)).astype(F32).astype(BF)


ROOT_HALF = 0.7071067811865476
DENSITY = 0.3989422804014327


def ffn_prepare(w_up, up_bias, w_down, up3, upt3, down3, bias_t):
    for f in range(4):
        block = w_up[:, 256 * f : 256 * f + 256]
        high, low = split(block)
        up3[f] = cat([high, low, high], 1)
        high, low = split(jnp.transpose(block))
        upt3[256 * f : 256 * f + 256, :] = cat([high, low, high], 1)
        high, low = split(w_down[256 * f : 256 * f + 256, :])
        down3[256 * f : 256 * f + 256, :] = cat([high, low, high], 1)
        bias = jnp.broadcast_to(up_bias[:, 256 * f : 256 * f + 256], (256, 256))
        bias_t[256 * f : 256 * f + 256, :] = jnp.transpose(bias)


def ffn_chunk(x, up, factor, gain, shift, up3, upt3, down3, bias_t, d_up_t, d_down, d_bias, first):
    unit, inverse = norm_stats(x)
    normed = unit * gain + shift
    grad = up * factor
    nh, nl = split(normed)
    gh, gl = split(grad)
    n_lanes, g_lanes = cat([nh, nh, nl], 1), cat([gh, gh, gl], 1)
    n_rows, g_rows = cat([nh, nh, nl], 0), cat([gh, gh, gl], 0)
    dn_t = None
    for f in range(4):
        rows = slice(256 * f, 256 * f + 256)
        pre = mm(upt3[rows, :], n_lanes, NT) + bias_t[rows, :]
        d_hidden = mm(down3[rows, :], g_lanes, NT)
        cdf = 0.5 * (1.0 + lax.erf(pre * ROOT_HALF))
        density = DENSITY * jnp.exp(-0.5 * pre * pre)
        hidden = pre * cdf
        d_pre = d_hidden * (cdf + pre * density)
        hh, hl = split(hidden)
        ph, pw = split(d_pre)
        part = mm(up3[f], cat([ph, ph, pw], 0), NN)
        dn_t = part if dn_t is None else dn_t + part
        down_part = mm(cat([hh, hl, hh], 1), g_rows, NN)
        up_part = mm(cat([ph, pw, ph], 1), n_rows, NN)
        bias_part = d_pre[:, :128] + d_pre[:, 128:]
        if first is True:
            d_down[rows, :] = down_part
            d_up_t[rows, :] = up_part
            d_bias[rows, :] = bias_part
        else:
            d_down[rows, :] += down_part
            d_up_t[rows, :] += up_part
            d_bias[rows, :] += bias_part
    d_normed = jnp.transpose(dn_t)
    d_x = norm_back(d_normed, unit, inverse, gain)
    return d_x, d_normed * unit, d_normed


def fold_rows(x):
    rows = x.shape[0]
    return jnp.sum(x.reshape(rows // 8, 8, x.shape[1]), axis=0)


def head_mask(head):
    lane = lax.broadcasted_iota(jnp.int32, (64, 128), 1)
    return (lane >> 5) == head


def spread_heads(x):
    zero = jnp.zeros_like(x)
    return cat([jnp.where(head_mask(h), x, zero) for h in range(4)], 0)


def pick_heads(full):
    out = full[0:64]
    for h in range(1, 4):
        out = jnp.where(head_mask(h), full[64 * h : 64 * h + 64], out)
    return out


def stacked(high, low, other_high, other_low, dims):
    two = mm(cat([high, low], 0), other_high, dims)
    return two[:64] + two[64:] + mm(high, other_low, dims)


def group_forward(q, k, v):
    qh, ql = split(q)
    kh, kl = split(k)
    vh, vl = split(v)
    scores = stacked(kh, kl, spread_heads(qh), spread_heads(ql), NT)
    scores = jnp.exp(scores - jnp.max(scores, axis=0, keepdims=True))
    p = scores * (1.0 / jnp.sum(scores, axis=0, keepdims=True))
    ph, pw = split(p)
    return p, pick_heads(mm(cat([ph, pw, ph], 0), cat([vh, vh, vl], 0), TN))


def group_backward(q, k, v, g, p):
    qh, ql = split(q)
    kh, kl = split(k)
    vh, vl = split(v)
    gh, gl = split(g)
    q_high, q_low = spread_heads(qh), spread_heads(ql)
    g_high, g_low = spread_heads(gh), spread_heads(gl)
    dp = stacked(vh, vl, g_high, g_low, NT)
    ph, pw = split(p)
    dv = stacked(ph, pw, g_high, g_low, NN)
    ds = p * (dp - jnp.sum(p * dp, axis=0, keepdims=True))
    sh, sw = split(ds)
    dk = stacked(sh, sw, q_high, q_low, NN)
    dq = pick_heads(mm(cat([sh, sw, sh], 0), cat([kh, kh, kl], 0), TN))
    return dq, dk, dv


def get(ref, part, rows):
    return cat([ref[2 * part, rows, :], ref[2 * part + 1, rows, :]], 1)


def put(ref, part, rows, x):
    ref[2 * part, rows, :] = x[:, :128]
    ref[2 * part + 1, rows, :] = x[:, 128:]

MESH = pl.DeviceIdType.MESH
UNROLL_FORWARD = 2
UNROLL_BACK = 4


def remote(src, dst, send, recv, device):
    return pltpu.make_async_remote_copy(
        src_ref=src, dst_ref=dst, send_sem=send, recv_sem=recv, device_id=(device,), device_id_type=MESH
    )


def arrived(ref, sem):
    pltpu.make_async_copy(ref, ref, sem).wait()


def at_rows(ref, start, size):
    return ref.at[pl.ds(pl.multiple_of(start, 8), size)]


def kernel(tokens, stored, upstream, drop_attn, drop_ffn, depth_keep, gain_one, shift_one, w_qkv, w_out,
           gain_two, shift_two, w_up, up_bias, w_down,
           through, back, ffn_all, att_all, vec_total,
           up3, upt3, down3, bias_t, d_bias, factor_ffn, factor_attn, branch,
           grid_tokens, grid_grad, d_grid,
           ffn_sum, ffn_half, slots_a, slots_b, slots_c,
           att_sum, att_half, att_slots, att_mine,
           vec, vec_slots,
           qkv, weights, mixed, d_qkv, d_mixed, unit_s, inverse_s, normed3, grad3,
           send, recv):
    me = lax.axis_index("rows")
    spot, core = me // 2, me % 2
    pair = me + 1 - 2 * core
    band, lane = me // 16, me % 16
    x, y, z = me // 32, (me // 8) % 4, (me // 2) % 4
    grad_scale = float(1024 * 128) ** (-0.5)
    steps = {"x": (x, 32), "y": (y, 8), "z": (z, 2)}

    def same_core(k):
        return ((spot + k) % 64) * 2 + core

    def along(axis, k):
        at, stride = steps[axis]
        return me + (((at + k) % 4) - at) * stride

    barrier = pltpu.get_barrier_semaphore()

    @pl.loop(1, 64)
    def _(k):
        pl.semaphore_signal(barrier, inc=1, device_id=(same_core(k),), device_id_type=MESH)

    pl.semaphore_signal(barrier, inc=1, device_id=(pair,), device_id_type=MESH)

    ffn_prepare(w_up, up_bias, w_down, up3, upt3, down3, bias_t)
    selector = make_selector()
    zeros = jnp.zeros((2, 1024), jnp.int32)
    tile = lax.broadcasted_iota(jnp.int32, (128, 1024), 0)
    column = lax.broadcasted_iota(jnp.int32, (128, 1024), 1)
    widen = (tile == (column >> 3)).astype(F32).astype(BF)
    flags = [
        mm(jnp.broadcast_to(depth_keep[n, pl.ds(me // 8, 1), :].astype(F32), (8, 128)).astype(BF), widen, NN)[0:1].astype(jnp.int32)
        for n in range(2)
    ]
    for n, (words, factor) in enumerate(((drop_attn, factor_attn), (drop_ffn, factor_ffn))):
        kept = keep_factor(cat([words[0], zeros], 0), flags[n], selector)
        factor[...] = kept.reshape(8, 128, D)

    def piece(ref, who):
        return ref.at[:, pl.ds(pl.multiple_of(16 * who, 16), 16), :]

    ffn_sum[...] = jnp.zeros_like(ffn_sum)
    d_bias[...] = jnp.zeros_like(d_bias)
    vec[...] = jnp.zeros_like(vec)
    d_up_t, d_down = ffn_sum.at[0:1024], ffn_sum.at[1024:2048]

    def send_branch(who):
        remote(piece(branch, who), grid_grad.at[band], send.at[1], recv.at[1], who * 16 + lane).start()

    pl.semaphore_wait(barrier, 64)
    pltpu.make_async_copy(piece(tokens, band), grid_tokens.at[band], recv.at[0]).start()

    @pl.loop(1, 8)
    def _(k):
        who = (band + k) % 8
        remote(piece(tokens, who), grid_tokens.at[band], send.at[0], recv.at[0], who * 16 + lane).start()

    @pl.loop(0, 4)
    def _(s):
        offset = 2 - s + 3 * (s // 2) - 2 * (s // 3)
        q = (band // 2 + offset) % 4
        cols = pl.ds(pl.multiple_of(q * 32, 32), 32)
        up = upstream[:, cols, :].reshape(256, D)
        d_x, d_gain, d_shift = ffn_chunk(
            stored[:, cols, :].reshape(256, D), up, factor_ffn[:, cols, :].reshape(256, D),
            gain_two[...], shift_two[...], up3, upt3, down3, bias_t, d_up_t, d_down, d_bias, False)
        total = up + d_x
        through[:, cols, :] = total.reshape(8, 32, D)
        branch[:, cols, :] = (total * factor_attn[:, cols, :].reshape(256, D)).reshape(8, 32, D)
        vec[0:1, :] += jnp.sum(d_gain, axis=0, keepdims=True)
        vec[1:2, :] += jnp.sum(d_shift, axis=0, keepdims=True)

        @pl.when(s < 3)
        def _():
            send_branch(2 * q)
            send_branch(2 * q + 1)

        @pl.when(s == 3)
        def _():
            send_branch(band + 1 - 2 * (band % 2))
            pltpu.make_async_copy(piece(branch, band), grid_grad.at[band], recv.at[1]).start()

    for f in range(4):
        vec[2 + f : 3 + f, :] = jnp.sum(jnp.transpose(d_bias[256 * f : 256 * f + 256, :]), axis=0, keepdims=True)

    def vec_start(n, axis):
        at = core if axis == "core" else steps[axis][0]
        pltpu.make_async_copy(vec, vec_slots.at[n, at], recv.at[16 + n]).start()
        for k in range(1, 2 if axis == "core" else 4):
            to = pair if axis == "core" else along(axis, k)
            remote(vec, vec_slots.at[n, at], send.at[16 + n], recv.at[16 + n], to).start()

    def vec_finish(n, axis):
        if axis == "core":
            arrived(vec_slots.at[n, 0:2], recv.at[16 + n])
            arrived(vec_slots.at[n, 0], send.at[16 + n])
            return vec_slots[n, 0] + vec_slots[n, 1]
        arrived(vec_slots.at[n], recv.at[16 + n])
        arrived(vec_slots.at[n, 0:3], send.at[16 + n])
        return (vec_slots[n, 0] + vec_slots[n, 1]) + (vec_slots[n, 2] + vec_slots[n, 3])

    mine = core * 1024
    ffn_pair = remote(at_rows(ffn_sum, (1 - core) * 1024, 1024), ffn_half, send.at[2], recv.at[2], pair)
    ffn_pair.start()
    orders = (("z", "x", "y"), ("y", "z", "x"))
    sizes = (128, 32, 8)
    slots = (slots_a, slots_b, slots_c)

    def block_start(part, step):
        start = 512 * part
        for n in range(step):
            start = start + steps[orders[part][n]][0] * sizes[n]
        return start

    def ffn_scatter_start(step):
        for part in range(2):
            axis = orders[part][step]
            sem = 24 + 3 * part + step
            for k in range(1, 4):
                to = (steps[axis][0] + k) % 4
                rows = at_rows(ffn_half, block_start(part, step) + to * sizes[step], sizes[step])
                remote(rows, slots[step].at[part, k - 1], send.at[sem], recv.at[sem], along(axis, k)).start()

    def ffn_scatter_finish(step):
        for part in range(2):
            arrived(slots[step].at[part], recv.at[24 + 3 * part + step])
            rows = pl.ds(pl.multiple_of(block_start(part, step + 1), 8), sizes[step])
            total = ffn_half[rows, :] + slots[step][part, 0] + slots[step][part, 1] + slots[step][part, 2]
            if step < 2:
                ffn_half[rows, :] = total
            else:
                ffn_all[pl.ds(pl.multiple_of(mine + block_start(part, 3), 8), 8), :] = total * grad_scale

    def ffn_gather_start(step):
        for part in range(2):
            sem = 30 + 3 * part + step
            rows = at_rows(ffn_all, mine + block_start(part, step + 1), sizes[step])
            for k in range(1, 4):
                remote(rows, rows, send.at[sem], recv.at[sem], along(orders[part][step], k)).start()

    def ffn_gather_finish(step):
        for part in range(2):
            arrived(slots[step].at[part], recv.at[30 + 3 * part + step])

    scale = HD ** (-0.5)
    wh, wl = split(w_qkv[...])
    w_rows = cat([wh, wh, wl], 0)
    arrived(grid_tokens, recv.at[0])
    for c in range(4):
        rows = slice(256 * c, 256 * c + 256)
        unit, inverse = norm_stats(grid_tokens[2 * c : 2 * c + 2].reshape(256, D))
        unit_s[rows, :] = unit
        inverse_s[rows, :] = jnp.broadcast_to(inverse, (256, 128))
        normed = unit * gain_one[...] + shift_one[...]
        nh, nl = split(jnp.transpose(normed))
        normed3[c] = cat([nh, nl, nh], 1)
        nh, nl = split(normed)
        out = mm(cat([nh, nl, nh], 1), w_rows, NN)
        put(qkv, 0, rows, out[:, :256] * scale)
        put(qkv, 1, rows, out[:, 256:512])
        put(qkv, 2, rows, out[:, 512:])

    ffn_pair.wait()
    ffn_half[...] += ffn_sum[pl.ds(pl.multiple_of(mine, 8), 1024), :]
    ffn_scatter_start(0)

    @pl.loop(0, 16 // UNROLL_FORWARD)
    def _(b):
        for n in range(UNROLL_FORWARD):
            at = b * UNROLL_FORWARD + n
            own = pl.ds(at, 64, stride=16)
            for h in range(2):
                p, m = group_forward(qkv[h, own, :], qkv[2 + h, own, :], qkv[4 + h, own, :])
                weights[h, at] = p
                mixed[h, own, :] = m

    oh, ol = split(w_out[...])
    o_lanes = cat([oh, oh, ol], 1)
    arrived(grid_grad, recv.at[1])
    for c in range(4):
        rows = slice(256 * c, 256 * c + 256)
        gh, gl = split(grid_grad[2 * c : 2 * c + 2].reshape(256, D))
        grad3[c] = cat([gh, gh, gl], 0)
        put(d_mixed, 0, rows, mm(cat([gh, gl, gh], 1), o_lanes, NT))

    def groups_back(h, b):
        for n in range(UNROLL_BACK):
            at = b * UNROLL_BACK + n
            own = pl.ds(at, 64, stride=16)
            dq, dk, dv = group_backward(
                qkv[h, own, :], qkv[2 + h, own, :], qkv[4 + h, own, :], d_mixed[h, own, :], weights[h, at])
            d_qkv[h, own, :] = dq * scale
            d_qkv[2 + h, own, :] = dk
            d_qkv[4 + h, own, :] = dv

    def weight_grads(h):
        for c in range(4):
            rows = slice(256 * c, 256 * c + 256)
            dh, dl = split(cat([d_qkv[2 * i + h, rows, :] for i in range(3)], 1))
            part = mm(normed3[c], cat([dh, dh, dl], 0), NN)
            mh, ml = split(jnp.transpose(mixed[h, rows, :]))
            part_o = mm(cat([mh, ml, mh], 1), grad3[c], NN)
            blocks = [part[:, 0:128], part[:, 128:256], part[:, 256:384], cat([part_o[:, :128], part_o[:, 128:]], 0)]
            for n, block in enumerate(blocks):
                if c == 0:
                    att_sum[h, 256 * n : 256 * n + 256, :] = block
                else:
                    att_sum[h, 256 * n : 256 * n + 256, :] += block

    def att_pair_copy(h):
        return remote(at_rows(att_sum.at[h], (1 - core) * 512, 512), att_half.at[h], send.at[9 + h], recv.at[9 + h], pair)

    def att_scatter_start(h):
        att_pair_copy(h).wait()
        att_half[h] += att_sum[h, pl.ds(pl.multiple_of(core * 512, 8), 512), :]

        @pl.loop(1, 64)
        def _(k):
            rows = at_rows(att_half.at[h], ((spot + k) % 64) * 8, 8)
            remote(rows, att_slots.at[h, k - 1], send.at[11 + h], recv.at[11 + h], same_core(k)).start()

    def att_gather_start(h):
        arrived(att_slots.at[h], recv.at[11 + h])
        own = att_half[h, pl.ds(pl.multiple_of(spot * 8, 8), 8), :]
        att_mine[h] = (own + jnp.sum(att_slots[h], axis=0)) * grad_scale
        rows = at_rows(att_all.at[h], core * 512 + spot * 8, 8)
        pltpu.make_async_copy(att_mine.at[h], rows, recv.at[13 + h]).start()

        @pl.loop(1, 64)
        def _(k):
            remote(att_mine.at[h], rows, send.at[13 + h], recv.at[13 + h], same_core(k)).start()

    def att_swap_copy(h):
        rows = at_rows(att_all.at[h], core * 512, 512)
        return remote(rows, rows, send.at[22 + h], recv.at[22 + h], pair)

    def groups_range(h, first, count):
        @pl.loop(first // UNROLL_BACK, (first + count) // UNROLL_BACK)
        def _(b):
            groups_back(h, b)

    w_lanes = cat([wh, wh, wl], 1)

    def token_grads(g):
        cols = slice(8 * g, 8 * g + 8)
        d_gain = jnp.zeros((8, D), F32)
        d_shift = jnp.zeros((8, D), F32)
        for c in range(2):
            rows = slice(512 * c, 512 * c + 512)

            def part(block):
                return block.reshape(32, 16, -1)[:, cols].reshape(256, -1)

            dh, dl = split(cat([part(d_qkv[i, rows, :]) for i in range(6)], 1))
            dn = mm(cat([dh, dl, dh], 1), w_lanes, NT)
            unit = part(unit_s[rows, :])
            inverse = part(inverse_s[rows, :])[:, 0:1]
            d_x = norm_back(dn, unit, inverse, gain_one[...])
            d_grid[g, 4 * c : 4 * c + 4] = d_x.reshape(4, 8, 8, D)
            d_gain += fold_rows(dn * unit)
            d_shift += fold_rows(dn)

        def home(who):
            return back.at[:, pl.ds(pl.multiple_of(16 * who + 8 * g, 8), 8), :]

        sem = (15, 3)[g]
        pltpu.make_async_copy(d_grid.at[g, band], home(band), recv.at[sem]).start()

        @pl.loop(1, 8)
        def _(k):
            who = (band + k) % 8
            remote(d_grid.at[g, who], home(band), send.at[sem], recv.at[sem], who * 16 + lane).start()

        return d_gain, d_shift

    groups_range(0, 0, 16)
    ffn_scatter_finish(0)
    ffn_scatter_start(1)
    weight_grads(0)
    att_pair_copy(0).start()
    groups_range(1, 0, 8)
    ffn_scatter_finish(1)
    ffn_scatter_start(2)
    att_scatter_start(0)
    gain_0, shift_0 = token_grads(0)
    vec[6:7, :] = jnp.sum(gain_0, axis=0, keepdims=True)
    vec[7:8, :] = jnp.sum(shift_0, axis=0, keepdims=True)
    groups_range(1, 8, 8)
    ffn_scatter_finish(2)
    ffn_gather_start(2)
    gain_1, shift_1 = token_grads(1)
    vec[6:7, :] += jnp.sum(gain_1, axis=0, keepdims=True)
    vec[7:8, :] += jnp.sum(shift_1, axis=0, keepdims=True)
    vec_start(0, "core")
    ffn_gather_finish(2)
    ffn_gather_start(1)
    att_gather_start(0)
    weight_grads(1)
    att_pair_copy(1).start()
    ffn_gather_finish(1)
    ffn_gather_start(0)
    vec[...] = vec_finish(0, "core")
    vec_start(1, "x")
    att_scatter_start(1)
    arrived(at_rows(att_all.at[0], core * 512, 512), recv.at[13])
    att_swap_copy(0).start()
    vec[...] = vec_finish(1, "x")
    vec_start(2, "y")
    att_gather_start(1)
    vec[...] = vec_finish(2, "y")
    vec_start(3, "z")
    ffn_gather_finish(0)
    ffn_rows = at_rows(ffn_all, mine, 1024)
    ffn_swap = remote(ffn_rows, ffn_rows, send.at[20], recv.at[20], pair)
    ffn_swap.start()
    vec_total[...] = vec_finish(3, "z") * grad_scale
    arrived(at_rows(att_all.at[1], core * 512, 512), recv.at[14])
    att_swap_copy(1).start()
    arrived(d_grid.at[0], recv.at[15])
    arrived(d_grid.at[1], recv.at[3])
    arrived(grid_tokens.at[0:7], send.at[0])
    arrived(grid_grad.at[0:7], send.at[1])
    for part in range(2):
        for step in range(3):
            arrived(slots[step].at[part], send.at[24 + 3 * part + step])
            arrived(slots[step].at[part], send.at[30 + 3 * part + step])
    for h in range(2):
        arrived(att_slots.at[h], send.at[11 + h])
        arrived(att_slots.at[h], send.at[13 + h])
    arrived(d_grid.at[0, 0:7], send.at[15])
    arrived(d_grid.at[1, 0:7], send.at[3])
    ffn_swap.wait()
    att_swap_copy(0).wait()
    att_swap_copy(1).wait()


def finish_kernel(through, back, ffn_all, att_all, vec,
                  result, out_gain_one, out_shift_one, out_qkv, out_out, out_gain_two, out_shift_two, out_up, out_bias, out_down):
    result[...] = through[...] + back[...]
    out_gain_two[...] = vec[0:1, :]
    out_shift_two[...] = vec[1:2, :]
    out_gain_one[...] = vec[6:7, :]
    out_shift_one[...] = vec[7:8, :]
    for f in range(4):
        cols = slice(256 * f, 256 * f + 256)
        out_bias[:, cols] = vec[2 + f : 3 + f, :]
        out_up[:, cols] = jnp.transpose(ffn_all[cols, :])
        out_down[cols, :] = ffn_all[1024 + 256 * f : 1280 + 256 * f, :]
    for h in range(2):
        for n in range(3):
            out_qkv[:, 256 * n + 128 * h : 256 * n + 128 * h + 128] = att_all[h, 256 * n : 256 * n + 256, :]
        for n in range(2):
            out_out[128 * h : 128 * h + 128, 128 * n : 128 * n + 128] = att_all[h, 768 + 128 * n : 896 + 128 * n, :]


VM = pl.BlockSpec(memory_space=pltpu.VMEM)
HB = pl.BlockSpec(memory_space=pl.ANY)
LIMIT = 62 * 1024 * 1024


def shape(*dims):
    return jax.ShapeDtypeStruct(dims, F32)


def local(tokens, stored, upstream, drop_attn, drop_ffn, depth_keep, gain_one, shift_one, w_qkv, w_out,
          gain_two, shift_two, w_up, up_bias, w_down):
    def v(*dims):
        return pltpu.VMEM(dims, F32)

    def b(*dims):
        return pltpu.VMEM(dims, BF)

    parts = pl.pallas_call(
        kernel,
        out_shape=(shape(8, 128, D), shape(8, 128, D), shape(2048, D), shape(2, 1024, 128), shape(8, D)),
        in_specs=[HB] + [VM] * 14,
        out_specs=(VM,) * 5,
        scratch_shapes=[
            b(4, 256, 768), b(1024, 768), b(1024, 768),
            v(1024, 256), v(1024, 128), v(8, 128, D), v(8, 128, D), v(8, 128, D),
            v(8, 8, 16, D), v(8, 8, 16, D), v(2, 8, 8, 8, D),
            v(2048, D), v(1024, D), v(2, 3, 128, D), v(2, 3, 32, D), v(2, 3, 8, D),
            v(2, 1024, 128), v(2, 512, 128), v(2, 63, 8, 128), v(2, 8, 128),
            v(8, D), v(4, 4, 8, D),
            v(6, 1024, 128), v(2, 16, 64, 256), v(2, 1024, 128), v(6, 1024, 128), v(2, 1024, 128),
            v(1024, 256), v(1024, 128), b(4, 256, 768), b(4, 768, 256),
            pltpu.SemaphoreType.DMA((36,)), pltpu.SemaphoreType.DMA((36,))],
        compiler_params=pltpu.CompilerParams(vmem_limit_bytes=LIMIT, collective_id=0, has_side_effects=True),
        name="block_back",
    )(tokens.reshape(8, 128, D), stored.reshape(8, 128, D), upstream.reshape(8, 128, D), drop_attn, drop_ffn, depth_keep,
      gain_one[None], shift_one[None], w_qkv, w_out, gain_two[None], shift_two[None], w_up, up_bias[None], w_down)
    outs = pl.pallas_call(
        finish_kernel,
        out_shape=(shape(8, 128, D), shape(1, D), shape(1, D), shape(D, 768), shape(D, D), shape(1, D), shape(1, D),
                   shape(D, FF), shape(1, FF), shape(FF, D)),
        in_specs=[VM] * 5,
        out_specs=(VM,) * 10,
        compiler_params=pltpu.CompilerParams(vmem_limit_bytes=LIMIT),
        name="finish",
    )(*parts)
    result, gain_one, shift_one, d_qkv, d_out, gain_two, shift_two, d_up, bias, d_down = outs
    return (result.reshape(1, 1024, D), gain_one[0], shift_one[0], d_qkv, d_out, gain_two[0], shift_two[0], d_up, bias[0], d_down)


def solution(mesh):
    banded = P("rows", None, None)
    return jax.shard_map(
        local,
        mesh=mesh,
        in_specs=(banded,) * 5 + (P(),) * 10,
        out_specs=(banded,) + (P(),) * 9,
        check_vma=False,
    )
```

time: 121 us -> 104 us (0.86)
  Pallas kernels: 110 us -> 101 us
  local copies, waits for them, and re-layouts: 10.7 us -> 2.92 us
    pallas_call x1 -> x2, Pallas kernels: 110 us -> 101 us  [the longest x1 95.6 us: local(): pl.pallas_call(kernel, out_shape=(shape(8, 128, D), shape(8, 128, D), sha...]
    unnamed x29 -> x2, local copies, waits for them, and re-layouts: 10.7 us -> 2.92 us
where the time goes in v2:
time: 104 us
  Pallas kernels  101 us (97%)
  local copies, waits for them, and re-layouts  2.92 us (3%)
    pallas_call x1, Pallas kernels, local(): pl.pallas_call(kernel, out_shape=(shape(8, 128, D), shape(8, 128, D), sha...  95.6 us
    pallas_call x1, Pallas kernels, local(): pl.pallas_call(finish_kernel, out_shape=(shape(8, 128, D), shape(1, D), s...  4.92 us
    unnamed x2, local copies, waits for them, and re-layouts  2.92 us

profile of v2, /device:TPU:1, one launch (start us, length us, event | category | flops | bytes accessed | tf_op | source)
XLA Modules:
  0.0 104.1 jit_solution(12602428472265113070)
XLA Ops:
  0.6 1.5 %copy.25.drop_attn = s32[1,14,1024]{2,1,0:T(8,128)} copy(s32[1,14,1024]{2,0,1:T(1,128)} %param.18) | data formatting | bytes 114688 | tf_op args[3]
  2.1 1.5 %copy.26.drop_ffn = s32[1,14,1024]{2,1,0:T(8,128)} copy(s32[1,14,1024]{2,0,1:T(1,128)} %param.19) | data formatting | bytes 114688 | tf_op args[4]
  3.6 95.6 %block_back.1 = (f32[8,128,256]{2,1,0:T(8,128)}, f32[8,128,256]{2,1,0:T(8,128)}, f32[2048,256]{1,0:T(8,128)}, f32[2,1024,128]{2,1,0:T(8,128)}, f32[8,256]{1,0:T(8,128)}) custom-call(f32[8,128,256]{2,1,0:T(8,128)} %bitcast.14, f32[8,128,256]{2,1,0:T(8,128)} %bitcast.15, f32[8,128,256]{2,1,0:T(8,128)} %bitcast.16, s32[1,14,1024]{2,1,0:T(8,128)} %copy.25.drop_attn, ...), custom_call_target="tpu_custom_call" | custom-call | tf_op jit(solution)/shard_map/block_back/pallas_call | solution.py:584
  99.2 4.9 %finish.1 = (f32[8,128,256]{2,1,0:T(8,128)}, f32[1,256]{1,0:T(1,128)}, f32[1,256]{1,0:T(1,128)}, f32[256,768]{1,0:T(8,128)}, f32[256,256]{1,0:T(8,128)}, /*index...) custom-call(f32[8,128,256]{2,1,0:T(8,128)} %get-tuple-element.25.through, ...), custom_call_target="tpu_custom_call" | custom-call | tf_op jit(solution)/shard_map/finish/pallas_call | solution.py:603

commit v3 on v2

--- a/solution.py
+++ b/solution.py
@@ -182,8 +182,11 @@
     ref[2 * part + 1, rows, :] = x[:, 128:]
 
 MESH = pl.DeviceIdType.MESH
-UNROLL_FORWARD = 2
-UNROLL_BACK = 4
+UNROLL_FORWARD = 4
+UNROLL_BACK = 2
+ATT_DIRECT = (False, True)
+FFN_ORDERS = (("z", "x", "y"), ("z", "y", "x"))
+ATT_ORDERS = (("z", "x", "y"), ("z", "y", "x"))
 
 
 def remote(src, dst, send, recv, device):
@@ -205,7 +208,7 @@
            through, back, ffn_all, att_all, vec_total,
            up3, upt3, down3, bias_t, d_bias, factor_ffn, factor_attn, branch,
            grid_tokens, grid_grad, d_grid,
-           ffn_sum, ffn_half, slots_a, slots_b, slots_c,
+           ffn_sum, ffn_half, slots_a, slots_b, slots_c, slots_d, slots_e, slots_f,
            att_sum, att_half, att_slots, att_mine,
            vec, vec_slots,
            qkv, weights, mixed, d_qkv, d_mixed, unit_s, inverse_s, normed3, grad3,
@@ -218,8 +221,16 @@
     grad_scale = float(1024 * 128) ** (-0.5)
     steps = {"x": (x, 32), "y": (y, 8), "z": (z, 2)}
 
+    way = 1
+
+    def other_spot(k):
+        return (spot + way * k + 64) % 64
+
+    def other_band(k):
+        return (band + way * k + 8) % 8
+
     def same_core(k):
-        return ((spot + k) % 64) * 2 + core
+        return other_spot(k) * 2 + core
 
     def along(axis, k):
         at, stride = steps[axis]
@@ -243,8 +254,8 @@
         mm(jnp.broadcast_to(depth_keep[n, pl.ds(me // 8, 1), :].astype(F32), (8, 128)).astype(BF), widen, NN)[0:1].astype(jnp.int32)
         for n in range(2)
     ]
-    for n, (words, factor) in enumerate(((drop_attn, factor_attn), (drop_ffn, factor_ffn))):
-        kept = keep_factor(cat([words[0], zeros], 0), flags[n], selector)
+    for which, (words, factor) in enumerate(((drop_attn, factor_attn), (drop_ffn, factor_ffn))):
+        kept = keep_factor(cat([words[n] for n in range(14)] + [zeros], 0), flags[which], selector)
         factor[...] = kept.reshape(8, 128, D)
 
     def piece(ref, who):
@@ -257,14 +268,6 @@
 
     def send_branch(who):
         remote(piece(branch, who), grid_grad.at[band], send.at[1], recv.at[1], who * 16 + lane).start()
-
-    pl.semaphore_wait(barrier, 64)
-    pltpu.make_async_copy(piece(tokens, band), grid_tokens.at[band], recv.at[0]).start()
-
-    @pl.loop(1, 8)
-    def _(k):
-        who = (band + k) % 8
-        remote(piece(tokens, who), grid_tokens.at[band], send.at[0], recv.at[0], who * 16 + lane).start()
 
     @pl.loop(0, 4)
     def _(s):
@@ -281,6 +284,16 @@
         vec[0:1, :] += jnp.sum(d_gain, axis=0, keepdims=True)
         vec[1:2, :] += jnp.sum(d_shift, axis=0, keepdims=True)
 
+        @pl.when(s == 0)
+        def _():
+            pl.semaphore_wait(barrier, 64)
+            pltpu.make_async_copy(piece(tokens, band), grid_tokens.at[band], recv.at[0]).start()
+
+            @pl.loop(1, 8)
+            def _(k):
+                who = other_band(k)
+                remote(piece(tokens, who), grid_tokens.at[band], send.at[0], recv.at[0], who * 16 + lane).start()
+
         @pl.when(s < 3)
         def _():
             send_branch(2 * q)
@@ -313,45 +326,75 @@
     mine = core * 1024
     ffn_pair = remote(at_rows(ffn_sum, (1 - core) * 1024, 1024), ffn_half, send.at[2], recv.at[2], pair)
     ffn_pair.start()
-    orders = (("z", "x", "y"), ("y", "z", "x"))
-    sizes = (128, 32, 8)
-    slots = (slots_a, slots_b, slots_c)
-
-    def block_start(part, step):
-        start = 512 * part
-        for n in range(step):
-            start = start + steps[orders[part][n]][0] * sizes[n]
-        return start
-
-    def ffn_scatter_start(step):
-        for part in range(2):
-            axis = orders[part][step]
-            sem = 24 + 3 * part + step
+    class AxisSum:
+        def __init__(self, half, total, base, total_base, order, sizes, slots, sem):
+            self.half, self.total, self.base, self.total_base = half, total, base, total_base
+            self.order, self.sizes, self.slots, self.sem = order, sizes, slots, sem
+
+        def block(self, step):
+            start = 0
+            for n in range(step):
+                start = start + steps[self.order[n]][0] * self.sizes[n]
+            return start
+
+        def scatter_start(self, step):
+            axis, sem = self.order[step], self.sem + step
             for k in range(1, 4):
                 to = (steps[axis][0] + k) % 4
-                rows = at_rows(ffn_half, block_start(part, step) + to * sizes[step], sizes[step])
-                remote(rows, slots[step].at[part, k - 1], send.at[sem], recv.at[sem], along(axis, k)).start()
+                rows = at_rows(self.half, self.base + self.block(step) + to * self.sizes[step], self.sizes[step])
+                remote(rows, self.slots[step].at[k - 1], send.at[sem], recv.at[sem], along(axis, k)).start()
+
+        def scatter_finish(self, step):
+            slots = self.slots[step]
+            arrived(slots, recv.at[self.sem + step])
+            rows = pl.ds(pl.multiple_of(self.base + self.block(step + 1), 8), self.sizes[step])
+            summed = self.half[rows, :] + slots[0] + slots[1] + slots[2]
+            if step < 2:
+                self.half[rows, :] = summed
+            else:
+                rows = pl.ds(pl.multiple_of(self.total_base + self.block(3), 8), self.sizes[2])
+                self.total[rows, :] = summed * grad_scale
+
+        def gather_start(self, step):
+            sem = self.sem + 3 + step
+            rows = at_rows(self.total, self.total_base + self.block(step + 1), self.sizes[step])
+            for k in range(1, 4):
+                remote(rows, rows, send.at[sem], recv.at[sem], along(self.order[step], k)).start()
+
+        def gather_finish(self, step):
+            arrived(self.slots[step], recv.at[self.sem + 3 + step])
+
+        def drain(self):
+            for step in range(3):
+                arrived(self.slots[step], send.at[self.sem + step])
+                arrived(self.slots[step], send.at[self.sem + 3 + step])
+
+    ffn_sums = [
+        AxisSum(ffn_half, ffn_all, 512 * part, mine + 512 * part, FFN_ORDERS[part], (128, 32, 8),
+                [slots_a.at[part], slots_b.at[part], slots_c.at[part]], 24 + 6 * part)
+        for part in range(2)
+    ]
+    att_sums = [
+        AxisSum(att_half.at[h], att_all.at[h], 0, core * 512, ATT_ORDERS[h], (128, 32, 8),
+                [slots_d.at[h], slots_e.at[h], slots_f.at[h]], 36 + 6 * h)
+        for h in range(2)
+    ]
+
+    def ffn_scatter_start(step):
+        for part in ffn_sums:
+            part.scatter_start(step)
 
     def ffn_scatter_finish(step):
-        for part in range(2):
-            arrived(slots[step].at[part], recv.at[24 + 3 * part + step])
-            rows = pl.ds(pl.multiple_of(block_start(part, step + 1), 8), sizes[step])
-            total = ffn_half[rows, :] + slots[step][part, 0] + slots[step][part, 1] + slots[step][part, 2]
-            if step < 2:
-                ffn_half[rows, :] = total
-            else:
-                ffn_all[pl.ds(pl.multiple_of(mine + block_start(part, 3), 8), 8), :] = total * grad_scale
+        for part in ffn_sums:
+            part.scatter_finish(step)
 
     def ffn_gather_start(step):
-        for part in range(2):
-            sem = 30 + 3 * part + step
-            rows = at_rows(ffn_all, mine + block_start(part, step + 1), sizes[step])
-            for k in range(1, 4):
-                remote(rows, rows, send.at[sem], recv.at[sem], along(orders[part][step], k)).start()
+        for part in ffn_sums:
+            part.gather_start(step)
 
     def ffn_gather_finish(step):
-        for part in range(2):
-            arrived(slots[step].at[part], recv.at[30 + 3 * part + step])
+        for part in ffn_sums:
+            part.gather_finish(step)
 
     scale = HD ** (-0.5)
     wh, wl = split(w_qkv[...])
@@ -424,10 +467,13 @@
     def att_scatter_start(h):
         att_pair_copy(h).wait()
         att_half[h] += att_sum[h, pl.ds(pl.multiple_of(core * 512, 8), 512), :]
+        if not ATT_DIRECT[h]:
+            att_sums[h].scatter_start(0)
+            return
 
         @pl.loop(1, 64)
         def _(k):
-            rows = at_rows(att_half.at[h], ((spot + k) % 64) * 8, 8)
+            rows = at_rows(att_half.at[h], other_spot(k) * 8, 8)
             remote(rows, att_slots.at[h, k - 1], send.at[11 + h], recv.at[11 + h], same_core(k)).start()
 
     def att_gather_start(h):
@@ -471,73 +517,102 @@
             d_gain += fold_rows(dn * unit)
             d_shift += fold_rows(dn)
 
-        def home(who):
-            return back.at[:, pl.ds(pl.multiple_of(16 * who + 8 * g, 8), 8), :]
-
         sem = (15, 3)[g]
-        pltpu.make_async_copy(d_grid.at[g, band], home(band), recv.at[sem]).start()
+        pltpu.make_async_copy(d_grid.at[g, band], back.at[g, band], recv.at[sem]).start()
 
         @pl.loop(1, 8)
         def _(k):
-            who = (band + k) % 8
-            remote(d_grid.at[g, who], home(band), send.at[sem], recv.at[sem], who * 16 + lane).start()
+            who = other_band(k)
+            remote(d_grid.at[g, who], back.at[g, band], send.at[sem], recv.at[sem], who * 16 + lane).start()
 
         return d_gain, d_shift
 
-    groups_range(0, 0, 16)
+    def att_step(h, n):
+        if ATT_DIRECT[h]:
+            return
+        if n < 3:
+            att_sums[h].scatter_finish(n - 1)
+            att_sums[h].scatter_start(n)
+        elif n == 3:
+            att_sums[h].scatter_finish(2)
+            att_sums[h].gather_start(2)
+        else:
+            att_sums[h].gather_finish(6 - n)
+            att_sums[h].gather_start(5 - n)
+
+    def att_finish(h):
+        if ATT_DIRECT[h]:
+            arrived(at_rows(att_all.at[h], core * 512, 512), recv.at[13 + h])
+        else:
+            att_sums[h].gather_finish(0)
+        att_swap_copy(h).start()
+
+    groups_range(0, 0, 8)
     ffn_scatter_finish(0)
     ffn_scatter_start(1)
+    groups_range(0, 8, 8)
+    ffn_scatter_finish(1)
+    ffn_scatter_start(2)
     weight_grads(0)
     att_pair_copy(0).start()
+    ffn_scatter_finish(2)
+    ffn_gather_start(2)
     groups_range(1, 0, 8)
-    ffn_scatter_finish(1)
-    ffn_scatter_start(2)
+    ffn_gather_finish(2)
+    ffn_gather_start(1)
     att_scatter_start(0)
     gain_0, shift_0 = token_grads(0)
     vec[6:7, :] = jnp.sum(gain_0, axis=0, keepdims=True)
     vec[7:8, :] = jnp.sum(shift_0, axis=0, keepdims=True)
     groups_range(1, 8, 8)
-    ffn_scatter_finish(2)
-    ffn_gather_start(2)
+    ffn_gather_finish(1)
+    ffn_gather_start(0)
+    att_step(0, 1)
     gain_1, shift_1 = token_grads(1)
     vec[6:7, :] += jnp.sum(gain_1, axis=0, keepdims=True)
     vec[7:8, :] += jnp.sum(shift_1, axis=0, keepdims=True)
     vec_start(0, "core")
-    ffn_gather_finish(2)
-    ffn_gather_start(1)
-    att_gather_start(0)
+    att_step(0, 2)
+    if ATT_DIRECT[0]:
+        att_gather_start(0)
     weight_grads(1)
     att_pair_copy(1).start()
-    ffn_gather_finish(1)
-    ffn_gather_start(0)
     vec[...] = vec_finish(0, "core")
     vec_start(1, "x")
+    att_step(0, 3)
     att_scatter_start(1)
-    arrived(at_rows(att_all.at[0], core * 512, 512), recv.at[13])
-    att_swap_copy(0).start()
+    att_step(0, 4)
     vec[...] = vec_finish(1, "x")
     vec_start(2, "y")
-    att_gather_start(1)
+    att_step(1, 1)
+    att_step(0, 5)
     vec[...] = vec_finish(2, "y")
     vec_start(3, "z")
+    att_step(1, 2)
+    if ATT_DIRECT[1]:
+        att_gather_start(1)
     ffn_gather_finish(0)
     ffn_rows = at_rows(ffn_all, mine, 1024)
     ffn_swap = remote(ffn_rows, ffn_rows, send.at[20], recv.at[20], pair)
     ffn_swap.start()
+    att_step(1, 3)
+    att_step(1, 4)
+    att_finish(0)
     vec_total[...] = vec_finish(3, "z") * grad_scale
-    arrived(at_rows(att_all.at[1], core * 512, 512), recv.at[14])
-    att_swap_copy(1).start()
-    arrived(d_grid.at[0], recv.at[15])
-    arrived(d_grid.at[1], recv.at[3])
+    att_step(1, 5)
+    att_finish(1)
+    arrived(back.at[0], recv.at[15])
+    arrived(back.at[1], recv.at[3])
     arrived(grid_tokens.at[0:7], send.at[0])
     arrived(grid_grad.at[0:7], send.at[1])
-    for part in range(2):
-        for step in range(3):
-            arrived(slots[step].at[part], send.at[24 + 3 * part + step])
-            arrived(slots[step].at[part], send.at[30 + 3 * part + step])
+    for part in ffn_sums:
+        part.drain()
     for h in range(2):
-        arrived(att_slots.at[h], send.at[11 + h])
-        arrived(att_slots.at[h], send.at[13 + h])
+        if ATT_DIRECT[h]:
+            arrived(att_slots.at[h], send.at[11 + h])
+            arrived(att_slots.at[h], send.at[13 + h])
+        else:
+            att_sums[h].drain()
     arrived(d_grid.at[0, 0:7], send.at[15])
     arrived(d_grid.at[1, 0:7], send.at[3])
     ffn_swap.wait()
@@ -547,7 +622,10 @@
 
 def finish_kernel(through, back, ffn_all, att_all, vec,
                   result, out_gain_one, out_shift_one, out_qkv, out_out, out_gain_two, out_shift_two, out_up, out_bias, out_down):
-    result[...] = through[...] + back[...]
+    for who in range(8):
+        for g in range(2):
+            cols = slice(16 * who + 8 * g, 16 * who + 8 * g + 8)
+            result[:, cols, :] = through[:, cols, :] + back[g, who]
     out_gain_two[...] = vec[0:1, :]
     out_shift_two[...] = vec[1:2, :]
     out_gain_one[...] = vec[6:7, :]
@@ -583,22 +661,22 @@
 
     parts = pl.pallas_call(
         kernel,
-        out_shape=(shape(8, 128, D), shape(8, 128, D), shape(2048, D), shape(2, 1024, 128), shape(8, D)),
+        out_shape=(shape(8, 128, D), shape(2, 8, 8, 8, D), shape(2048, D), shape(2, 1024, 128), shape(8, D)),
         in_specs=[HB] + [VM] * 14,
         out_specs=(VM,) * 5,
         scratch_shapes=[
             b(4, 256, 768), b(1024, 768), b(1024, 768),
             v(1024, 256), v(1024, 128), v(8, 128, D), v(8, 128, D), v(8, 128, D),
             v(8, 8, 16, D), v(8, 8, 16, D), v(2, 8, 8, 8, D),
-            v(2048, D), v(1024, D), v(2, 3, 128, D), v(2, 3, 32, D), v(2, 3, 8, D),
+            v(2048, D), v(1024, D), v(2, 3, 128, D), v(2, 3, 32, D), v(2, 3, 8, D), v(2, 3, 128, 128), v(2, 3, 32, 128), v(2, 3, 8, 128),
             v(2, 1024, 128), v(2, 512, 128), v(2, 63, 8, 128), v(2, 8, 128),
             v(8, D), v(4, 4, 8, D),
             v(6, 1024, 128), v(2, 16, 64, 256), v(2, 1024, 128), v(6, 1024, 128), v(2, 1024, 128),
             v(1024, 256), v(1024, 128), b(4, 256, 768), b(4, 768, 256),
-            pltpu.SemaphoreType.DMA((36,)), pltpu.SemaphoreType.DMA((36,))],
+            pltpu.SemaphoreType.DMA((48,)), pltpu.SemaphoreType.DMA((48,))],
         compiler_params=pltpu.CompilerParams(vmem_limit_bytes=LIMIT, collective_id=0, has_side_effects=True),
         name="block_back",
-    )(tokens.reshape(8, 128, D), stored.reshape(8, 128, D), upstream.reshape(8, 128, D), drop_attn, drop_ffn, depth_keep,
+    )(tokens.reshape(8, 128, D), stored.reshape(8, 128, D), upstream.reshape(8, 128, D), drop_attn.transpose(1, 0, 2), drop_ffn.transpose(1, 0, 2), depth_keep,
       gain_one[None], shift_one[None], w_qkv, w_out, gain_two[None], shift_two[None], w_up, up_bias[None], w_down)
     outs = pl.pallas_call(
         finish_kernel,

time: 104 us -> 104 us (level)
  local copies, waits for them, and re-layouts: 2.92 us -> 0 us
  Pallas kernels: 101 us -> 103 us
    unnamed x2 -> x0, local copies, waits for them, and re-layouts: 2.92 us -> none
    pallas_call x1, Pallas kernels: 95.6 us -> 98.1 us  [local(): pl.pallas_call(kernel, out_shape=(shape(8, 128, D), shape(2, 8, 8, 8, D),...]
where the time goes in v3:
time: 104 us
  Pallas kernels  103 us (99%)
    pallas_call x1, Pallas kernels, local(): pl.pallas_call(kernel, out_shape=(shape(8, 128, D), shape(2, 8, 8, 8, D),...  98.1 us
    pallas_call x1, Pallas kernels, local(): pl.pallas_call(finish_kernel, out_shape=(shape(8, 128, D), shape(1, D), s...  4.92 us

profile of v3, /device:TPU:1, one launch (start us, length us, event | category | flops | bytes accessed | tf_op | source)
XLA Modules:
  0.0 103.7 jit_solution(16132345393450447358)
XLA Ops:
  0.6 98.1 %block_back.1 = (f32[8,128,256]{2,1,0:T(8,128)}, f32[2,8,8,8,256]{4,3,2,1,0:T(8,128)}, f32[2048,256]{1,0:T(8,128)}, f32[2,1024,128]{2,1,0:T(8,128)}, f32[8,256]{1,0:T(8,128)}) custom-call(f32[8,128,256]{2,1,0:T(8,128)} %bitcast.16, f32[8,128,256]{2,1,0:T(8,128)} %bitcast.17, f32[8,128,256]{2,1,0:T(8,128)} %bitcast.18, s32[14,1,1024]{2,1,0:T(1,128)} %bitcast.19, ...), custom_call_target="tpu_custom_call" | custom-call | tf_op jit(solution)/shard_map/block_back/pallas_call | solution.py:662
  98.8 4.9 %finish.1 = (f32[8,128,256]{2,1,0:T(8,128)}, f32[1,256]{1,0:T(1,128)}, f32[1,256]{1,0:T(1,128)}, f32[256,768]{1,0:T(8,128)}, f32[256,256]{1,0:T(8,128)}, /*index...) custom-call(f32[8,128,256]{2,1,0:T(8,128)} %get-tuple-element.25.through, ...), custom_call_target="tpu_custom_call" | custom-call | tf_op jit(solution)/shard_map/finish/pallas_call | solution.py:681
